TPU v7x, 32 devices: a whole 2x2x4 slice. The times are simulated.
32 devices in a mesh: groups: 2 (over y), dp: 4 (over z), tile: 4 (over x, core).
Axes of the slice: x: 2, y: 2, z: 4, core: 2. Of those that a mesh axis runs over, the one named last changes fastest.
Arguments:
- features: bfloat16 [8, 32, 128, 1024], P(('groups', 'dp'), 'tile'), parts along dimension 0, may hold values from -18 to 18
- cotangent: bfloat16 [8, 32, 128, 512], P(('groups', 'dp'), 'tile'), parts along dimension 0, may hold values from -6 to 6
- weight_first: bfloat16 [1024, 512], replicated, may hold values from -0.1875 to 0.1875
- weight_second: bfloat16 [512, 512], replicated, may hold values from -0.25 to 0.25
- cluster_id: int32 [8, 32, 128], P(('groups', 'dp'), 'tile'), parts along dimension 0, may hold values from 0 to 2047, as said below
- cluster_size: int32 [8, 2048], P(('groups', 'dp')), parts along dimension 0, may hold values from 1 to 3, as said below
Outputs:
- grad_features: bfloat16 [8, 32, 128, 1024], P(('groups', 'dp'), 'tile'), parts along dimension 0
- grad_first: float32 [2048, 512], P('groups'), parts along dimension 0
- grad_second: float32 [1024, 512], P('groups'), parts along dimension 0
There are 2 independent parts, one for each index of `groups`. A program takes and returns all parts, laid end to end along the dimension named above; an argument that names none is the same for every part. Nothing has to cross between parts.
Inputs may be any that keep to these rules, and one draw needn't show every extreme that they name: `cluster_id`: every one of the 2048 clusters has at least one tile in every slide. cluster_size[s, k] is the number of tiles of slide s whose cluster_id is k; in every slide some cluster reaches the maximum and some has a single tile.
All inputs are finite; a program needn't handle non-finite values.
Results may differ from a plain program's by a relative error of at most 0.011.
Values may be sent and summed in bfloat16 or wider, within the bound.
A program may use at most 128 MiB of HBM per device.

v0:
```python
import jax
import jax.numpy as jnp
from jax import lax
from jax.sharding import PartitionSpec as P


def extended(cells, sides, width):
    for axis, dim in sides:
        count = lax.axis_size(axis)
        ends = count - 1
        head = lax.slice_in_dim(cells, 0, width, axis=dim)
        tail = lax.slice_in_dim(cells, cells.shape[dim] - width, cells.shape[dim], axis=dim)
        cells = jnp.concatenate(
            [
                lax.ppermute(tail, axis, [(i, (i + 1) % count) for i in range(ends)]),
                cells,
                lax.ppermute(head, axis, [((i + 1) % count, i) for i in range(ends)]),
            ],
            axis=dim,
        )
    return cells


def rowbox(values):
    return values[:-2] + values[1:-1] + values[2:]


def colbox(values):
    padded = jnp.pad(values, ((0, 0), (1, 1), (0, 0)))
    return padded[:, :-2] + padded[:, 1:-1] + padded[:, 2:]


def spread_rows(global_rows, row_total, col_total):
    row_part = (
        3.0
        - (global_rows == 0).astype(jnp.float32)
        - (global_rows == row_total - 1).astype(jnp.float32)
    )
    col_index = jnp.arange(col_total)
    col_part = (
        3.0
        - (col_index == 0).astype(jnp.float32)
        - (col_index == col_total - 1).astype(jnp.float32)
    )
    return row_part[:, None] * col_part[None, :]


def propagate(values, members, member_sizes):
    band_rows, grid_cols, width = values.shape
    bands = lax.axis_size("tile")
    row_start = lax.axis_index("tile") * band_rows
    row_total = band_rows * bands
    global_rows = row_start + jnp.arange(band_rows)
    spread = spread_rows(global_rows, row_total, grid_cols)
    root = 1.0 / jnp.sqrt(spread + 1.0)
    scaled = (values.astype(jnp.float32) * root[..., None]).astype(jnp.bfloat16)
    padded = extended(scaled, (("tile", 0),), 1)
    spatial_mean = colbox(rowbox(padded.astype(jnp.float32))) / spread[..., None]
    widened = extended(spatial_mean, (("tile", 0),), 1)
    spatial = colbox(rowbox(widened))
    clusters = member_sizes.shape[0]
    sizes_float = member_sizes.astype(jnp.float32)
    piece_values = lax.all_gather(scaled, "tile", axis=0, tiled=True)
    piece_members = lax.all_gather(members, "tile", axis=0, tiled=True)
    totals = jax.ops.segment_sum(
        piece_values.reshape(-1, width).astype(jnp.float32),
        piece_members.reshape(-1),
        num_segments=clusters,
    )
    cluster_mean = (totals / sizes_float[:, None]).astype(jnp.bfloat16)
    picked = jnp.take(cluster_mean, members.reshape(-1), axis=0).reshape(values.shape)
    return (root[..., None] * (spatial + picked.astype(jnp.float32))).astype(jnp.bfloat16)


def local(features, cotangent, weight_first, weight_second, cluster_id, cluster_size):
    feats = features[0]
    band_rows, grid_cols, in_width = feats.shape
    hidden_width = weight_first.shape[1]
    out_width = weight_second.shape[1]
    members = cluster_id[0]
    member_sizes = cluster_size[0]
    flat_in = feats.reshape(-1, in_width)
    hidden_in = jnp.dot(flat_in, weight_first, preferred_element_type=jnp.float32).astype(
        jnp.bfloat16
    )
    hidden_grid = hidden_in.reshape(band_rows, grid_cols, hidden_width)
    pre_act = propagate(hidden_grid, members, member_sizes)
    back_second = propagate(cotangent[0], members, member_sizes)
    pre_flat = pre_act.reshape(-1, hidden_width).astype(jnp.float32)
    sigma = jax.nn.sigmoid(pre_flat)
    activated = (pre_flat * sigma).astype(jnp.bfloat16)
    back_flat = back_second.reshape(-1, out_width)
    grad_second = lax.dot_general(
        activated, back_flat, (((0,), (0,)), ((), ())), preferred_element_type=jnp.float32
    )
    upstream = lax.dot_general(
        back_flat, weight_second, (((1,), (1,)), ((), ())), preferred_element_type=jnp.float32
    )
    grad_pre = (upstream * sigma * (1.0 + pre_flat * (1.0 - sigma))).astype(jnp.bfloat16)
    back_first = propagate(
        grad_pre.reshape(band_rows, grid_cols, hidden_width), members, member_sizes
    )
    first_flat = back_first.reshape(-1, hidden_width)
    grad_first = lax.dot_general(
        flat_in, first_flat, (((0,), (0,)), ((), ())), preferred_element_type=jnp.float32
    )
    grad_feats = lax.dot_general(
        first_flat, weight_first, (((1,), (1,)), ((), ())), preferred_element_type=jnp.float32
    ).astype(jnp.bfloat16)
    grad_first, grad_second = lax.psum((grad_first, grad_second), ("dp", "tile"))
    return (grad_feats.reshape(1, band_rows, grid_cols, in_width), grad_first, grad_second)


def solution(mesh):
    in_specs = (
        P(("groups", "dp"), "tile", None, None),
        P(("groups", "dp"), "tile", None, None),
        P(),
        P(),
        P(("groups", "dp"), "tile", None),
        P(("groups", "dp"), None),
    )
    out_specs = (P(("groups", "dp"), "tile", None, None), P("groups", None), P("groups", None))
    return jax.shard_map(local, mesh=mesh, in_specs=in_specs, out_specs=out_specs, check_vma=False)
```

profile of v0, /device:TPU:0, one launch (start us, length us, event | category | flops | bytes accessed | tf_op | source)
XLA Modules:
  0.0 340.3 jit_solution(15276775889147698415)
XLA Ops:
  7.2 0.0 all-gather.5.cloned.1.call-start
  7.3 0.1 broadcast_multiply_fusion
  7.3 1.4 copy-done
  8.8 2.6 convolution_convert_fusion.1
  11.3 1.7 fusion.38
  13.1 0.0 all-gather.7.cloned.1.call-start
  13.1 0.7 all-gather.7.cloned.1.call-update
  13.9 1.0 fusion.63
  14.9 2.4 collective-permute-start
  17.3 1.3 collective-permute-start.1
  18.6 5.3 %collective-permute-start.4 = (bf16[1,128,512]{2,1,0:T(8,128)(2,1)S(1)}, bf16[1,128,512]{2,1,0:T(8,128)(2,1)S(1)}, u32[]{:S(2)}, u32[]{:S(2)}) collective-permute-start(bf16[1,128,512]{2,1,0:T(8,128)(2,1)S(1)} %get-tuple-element.22), channel_id=1, source_target_pairs={{0,1},{1,2},{2,3},{4,5},{5,6},{6,7},{8,9},{9,10},{10,11},{12,13},{... | collective-permute-start | bytes 393224 | tf_op jit(solution)/shard_map/ppermute | solution.py:15
  23.9 1.3 collective-permute-start.5
  25.2 3.1 collective-permute-done.5
  28.4 0.2 maximum_convert_fusion.1
  28.6 0.2 maximum_convert_fusion
  28.8 0.3 slice_add_fusion.2
  29.1 0.3 slice_add_fusion.4
  29.5 1.2 fusion.8
  30.8 8.6 %collective-permute-start.2 = (f32[1,128,512]{2,1,0:T(8,128)S(1)}, f32[1,128,512]{2,1,0:T(8,128)S(1)}, u32[]{:S(2)}, u32[]{:S(2)}) collective-permute-start(f32[1,128,512]{2,1,0:T(8,128)S(1)} %get-tuple-element.14), channel_id=1, source_target_pairs={{0,1},{1,2},{2,3},{4,5},{5,6},{6,7},{8,9},{9,10},{10,11},{12,13},{... | collective-permute-start | bytes 786440 | tf_op jit(solution)/shard_map/ppermute | solution.py:15
  39.4 1.3 collective-permute-start.3
  40.8 13.1 %all-gather = s32[1,32,128]{2,1,0:T(8,128)S(1)} all-gather(s32[1,8,128]{2,1,0:T(8,128)S(1)} %copy-done.13), channel_id=2, replica_groups=mesh['groups'=2,'dp'=4,'tile'=4] {'tile'}, dimensions={1}, use_global_device_ids=true | all-gather | bytes 20480 | tf_op jit(solution)/shard_map/all_gather | solution.py:64
  53.9 2.2 collective-permute-start.6
  56.1 1.3 collective-permute-start.7
  57.5 1.7 fusion.34
  59.2 0.4 collective-permute-done.7
  59.6 1.7 fusion.32
  61.3 27.8 %scatter_custom_fusion = f32[2048,512]{1,0:T(8,128)} fusion(s32[4096]{0:T(1024)S(1)} %bitcast.76, bf16[4096,512]{1,0:T(8,128)(2,1)} %bitcast.66, f32[]{:T(128)} %constant.6.clone.1), kind=kCustom, calls=%fused_computation.10 | custom fusion | flops 4194304 | bytes 8388612 | tf_op jit(solution)/shard_map/scatter-add | solution.py:65
  89.1 2.6 all-gather.7.cloned.1.call-done
  91.7 27.8 %scatter_custom_fusion.1 = f32[2048,512]{1,0:T(8,128)} fusion(s32[4096]{0:T(1024)S(1)} %bitcast.77, bf16[4096,512]{1,0:T(8,128)(2,1)} %bitcast.67, f32[]{:T(128)} %constant.6.clone.1), kind=kCustom, calls=%fused_computation.8 | custom fusion | flops 4194304 | bytes 8388612 | tf_op jit(solution)/shard_map/scatter-add | solution.py:65
  119.5 5.3 %divide_convert_fusion.2 = (bf16[2048,512]{1,0:T(8,128)(2,1)}, bf16[2048,512]{1,0:T(8,128)(2,1)}) fusion(f32[2048,512]{1,0:T(8,128)} %scatter_custom_fusion, f32[2048]{0:T(1024)S(1)} %bitcast.74, f32[2048,512]{1,0:T(8,128)} %scatter_custom_fusion.1), kind=kLoop, calls=%fused_computation.14 | loop fusion | flops 4194304 | bytes 12591104 | tf_op jit(solution)/shard_map/convert_element_type | solution.py:70
  124.7 5.8 %gather_fusion = bf16[1024,512]{1,0:T(8,128)(2,1)S(1)} fusion(bf16[2048,512]{1,0:T(8,128)(2,1)} %get-tuple-element.24, s32[1024]{0:T(1024)S(1)} %fusion.53), kind=kCustom, calls=%fused_computation.clone | custom fusion | bytes 2101248 | tf_op jit(solution)/shard_map/jit(_take)/gather | solution.py:71
  130.6 7.0 %gather_fusion.1 = bf16[1024,512]{1,0:T(8,128)(2,1)} fusion(bf16[2048,512]{1,0:T(8,128)(2,1)} %get-tuple-element.25, s32[1024]{0:T(1024)S(1)} %fusion.53), kind=kCustom, calls=%fused_computation.1.clone | custom fusion | bytes 2101248 | tf_op jit(solution)/shard_map/jit(_take)/gather | solution.py:71
  137.6 1.6 broadcast_select_fusion.2
  139.2 0.3 copy-done.5
  139.5 0.6 copy-done.6
  140.1 1.3 fusion.13
  141.5 1.2 fusion.48
  142.7 0.1 copy-done.11
  142.8 1.3 fusion.36
  144.1 0.0 all-reduce.9.cloned.1.call-start
  144.1 1.1 fusion.62
  145.2 3.7 %collective-permute-start.8 = (bf16[1,128,512]{2,1,0:T(8,128)(2,1)S(1)}, bf16[1,128,512]{2,1,0:T(8,128)(2,1)S(1)}, u32[]{:S(2)}, u32[]{:S(2)}) collective-permute-start(bf16[1,128,512]{2,1,0:T(8,128)(2,1)S(1)} %get-tuple-element.18), channel_id=1, source_target_pairs={{0,1},{1,2},{2,3},{4,5},{5,6},{6,7},{8,9},{9,10},{10,11},{12,13},{... | collective-permute-start | bytes 393224 | tf_op jit(solution)/shard_map/ppermute | solution.py:15
  148.9 1.3 collective-permute-start.9
  150.3 1.9 collective-permute-done.9
  152.2 0.2 maximum_convert_fusion.2
  152.4 0.3 slice_add_fusion
  152.8 0.5 fusion.24
  153.3 5.1 %collective-permute-start.10 = (f32[1,128,512]{2,1,0:T(8,128)S(1)}, f32[1,128,512]{2,1,0:T(8,128)S(1)}, u32[]{:S(2)}, u32[]{:S(2)}) collective-permute-start(f32[1,128,512]{2,1,0:T(8,128)S(1)} %get-tuple-element.12), channel_id=1, source_target_pairs={{0,1},{1,2},{2,3},{4,5},{5,6},{6,7},{8,9},{9,10},{10,11},{12,13},{... | collective-permute-start | bytes 786440 | tf_op jit(solution)/shard_map/ppermute | solution.py:15
  158.4 1.3 collective-permute-start.11
  159.8 1.8 convolution_bitcast_fusion.1
  161.5 0.4 collective-permute-done.11
  161.9 1.7 fusion.30
  163.6 19.8 %all-gather.9.cloned.1.call-done = bf16[32,128,512]{2,1,0:T(8,128)(2,1)} async-done(((bf16[8,128,512]{2,1,0:T(8,128)(2,1)}), bf16[32,128,512]{2,1,0:T(8,128)(2,1)}) %all-gather.9.cloned.1.call-update) | async-done | bytes 4194320 | tf_op jit(solution)/shard_map/all_gather | solution.py:63
  183.4 27.8 %scatter_custom_fusion.2 = f32[2048,512]{1,0:T(8,128)} fusion(s32[4096]{0:T(1024)S(1)} %bitcast.78, bf16[4096,512]{1,0:T(8,128)(2,1)} %bitcast.68, f32[]{:T(128)} %constant.6.clone.1), kind=kCustom, calls=%fused_computation.6 | custom fusion | flops 4194304 | bytes 8388612 | tf_op jit(solution)/shard_map/scatter-add | solution.py:65
  211.2 3.9 %divide_convert_fusion = bf16[2048,512]{1,0:T(8,128)(2,1)} fusion(f32[2048,512]{1,0:T(8,128)} %scatter_custom_fusion.2, f32[2048]{0:T(1024)S(1)} %bitcast.75), kind=kLoop, calls=%fused_computation.12 | loop fusion | flops 2097152 | bytes 6299648 | tf_op jit(solution)/shard_map/convert_element_type | solution.py:70
  215.1 5.8 %gather_fusion.2 = bf16[1024,512]{1,0:T(8,128)(2,1)S(1)} fusion(bf16[2048,512]{1,0:T(8,128)(2,1)} %divide_convert_fusion, s32[1024]{0:T(1024)S(1)} %fusion.53), kind=kCustom, calls=%fused_computation.2.clone | custom fusion | bytes 2101248 | tf_op jit(solution)/shard_map/jit(_take)/gather | solution.py:71
  220.9 0.2 broadcast_select_fusion
  221.2 1.4 copy-done.4
  222.5 0.7 fusion.29
  223.2 2.6 convolution_bitcast_fusion
  225.8 3.8 %convolution_convert_fusion = bf16[1024,1024]{1,0:T(8,128)(2,1)} fusion(bf16[1024,512]{1,0:T(8,128)(2,1)S(1)} %bitcast.64, bf16[1024,512]{1,0:T(8,128)(2,1)} %param.10), kind=kOutput, calls=%fused_computation.92 | convolution fusion | flops 1074790400 | bytes 4194304 | tf_op jit(solution)/shard_map/dot_general | solution.py:107
  229.7 100.2 %all-reduce.9.cloned.1.call-done = (f32[1024,512]{0,1:T(8,128)}, f32[512,512]{1,0:T(8,128)}) async-done(((f32[1024,512]{0,1:T(8,128)}, f32[512,512]{1,0:T(8,128)}), (f32[1024,512]{0,1:T(8,128)}, f32[512,512]{1,0:T(8,128)})) %all-reduce.9.cloned.1.call-update) | async-done | bytes 3145744 | tf_op jit(solution)/shard_map/psum | solution.py:110
  329.9 3.0 copy.12
  332.8 1.0 copy.16
  (49 shorter events, 0.3 us)
Async XLA Ops:
  7.2 1.6 copy-start
  7.2 54.1 %all-gather.5.cloned.1.call-start = ((), (), s32[]{:S(2)}) async-start(), calls=%async_computation | async-start | bytes 5242880 | tf_op jit(solution)/shard_map/all_gather | solution.py:63
  8.8 2.6 copy-start.7
  13.1 5.5 %copy-start.1 = (bf16[8,128,512]{2,1,0:T(8,128)(2,1)S(1)}, bf16[8,128,512]{2,1,0:T(8,128)(2,1)}, u32[]{:S(2)}) copy-start(bf16[8,128,512]{2,1,0:T(8,128)(2,1)} %get-tuple-element.31) | copy-start | bytes 3145732
  13.1 12.1 %copy-start.13 = (s32[1,8,128]{2,1,0:T(8,128)S(1)}, s32[1,8,128]{2,1,0:T(8,128)}, u32[]{:S(2)}) copy-start(s32[1,8,128]{2,1,0:T(8,128)} %param.12) | copy-start | bytes 12292
  13.1 78.6 %all-gather.7.cloned.1.call-start = ((), (), s32[]{:S(2)}) async-start(), calls=%async_computation.1 | async-start | bytes 5242880 | tf_op jit(solution)/shard_map/all_gather | solution.py:63
  13.8 169.5 %all-gather.9.cloned.1.call-start = ((), (), s32[]{:S(2)}) async-start(), calls=%async_computation.2 | async-start | bytes 5242880 | tf_op jit(solution)/shard_map/all_gather | solution.py:63
  14.9 13.7 %collective-permute-start = (bf16[1,128,512]{2,1,0:T(8,128)(2,1)S(1)}, bf16[1,128,512]{2,1,0:T(8,128)(2,1)S(1)}, u32[]{:S(2)}, u32[]{:S(2)}) collective-permute-start(bf16[1,128,512]{2,1,0:T(8,128)(2,1)S(1)} %get-tuple-element.20), channel_id=1, source_target_pairs={{0,1},{1,2},{2,3},{4,5},{5,6},{6,7},{8,9},{9,10},{10,11},{12,13},{... | collective-permute-start | bytes 393224 | tf_op jit(solution)/shard_map/ppermute | solution.py:15
  17.3 11.3 %collective-permute-start.1 = (bf16[1,128,512]{2,1,0:T(8,128)(2,1)S(1)}, bf16[1,128,512]{2,1,0:T(8,128)(2,1)S(1)}, u32[]{:S(2)}, u32[]{:S(2)}) collective-permute-start(bf16[1,128,512]{2,1,0:T(8,128)(2,1)S(1)} %get-tuple-element.21), channel_id=1, source_target_pairs={{1,0},{2,1},{3,2},{5,4},{6,5},{7,6},{9,8},{10,9},{11,10},{13,12},{... | collective-permute-start | bytes 393224 | tf_op jit(solution)/shard_map/ppermute | solution.py:17
  18.6 10.0 %copy-start.2 = (bf16[8,128,512]{2,1,0:T(8,128)(2,1)S(1)}, bf16[8,128,512]{2,1,0:T(8,128)(2,1)}, u32[]{:S(2)}) copy-start(bf16[8,128,512]{2,1,0:T(8,128)(2,1)} %get-tuple-element.30) | copy-start | bytes 3145732
  18.6 6.6 %collective-permute-start.4 = (bf16[1,128,512]{2,1,0:T(8,128)(2,1)S(1)}, bf16[1,128,512]{2,1,0:T(8,128)(2,1)S(1)}, u32[]{:S(2)}, u32[]{:S(2)}) collective-permute-start(bf16[1,128,512]{2,1,0:T(8,128)(2,1)S(1)} %get-tuple-element.22), channel_id=1, source_target_pairs={{0,1},{1,2},{2,3},{4,5},{5,6},{6,7},{8,9},{9,10},{10,11},{12,13},{... | collective-permute-start | bytes 393224 | tf_op jit(solution)/shard_map/ppermute | solution.py:15
  23.9 4.5 %collective-permute-start.5 = (bf16[1,128,512]{2,1,0:T(8,128)(2,1)S(1)}, bf16[1,128,512]{2,1,0:T(8,128)(2,1)S(1)}, u32[]{:S(2)}, u32[]{:S(2)}) collective-permute-start(bf16[1,128,512]{2,1,0:T(8,128)(2,1)S(1)} %get-tuple-element.23), channel_id=1, source_target_pairs={{1,0},{2,1},{3,2},{5,4},{6,5},{7,6},{9,8},{10,9},{11,10},{13,12},{... | collective-permute-start | bytes 393224 | tf_op jit(solution)/shard_map/ppermute | solution.py:17
  29.5 11.3 %copy-start.14 = (s32[1,2048]{1,0:T(1,128)S(1)}, s32[1,2048]{1,0:T(1,128)}, u32[]{:S(2)}) copy-start(s32[1,2048]{1,0:T(1,128)} %param.13) | copy-start | bytes 24580
  30.8 26.6 %collective-permute-start.2 = (f32[1,128,512]{2,1,0:T(8,128)S(1)}, f32[1,128,512]{2,1,0:T(8,128)S(1)}, u32[]{:S(2)}, u32[]{:S(2)}) collective-permute-start(f32[1,128,512]{2,1,0:T(8,128)S(1)} %get-tuple-element.14), channel_id=1, source_target_pairs={{0,1},{1,2},{2,3},{4,5},{5,6},{6,7},{8,9},{9,10},{10,11},{12,13},{... | collective-permute-start | bytes 786440 | tf_op jit(solution)/shard_map/ppermute | solution.py:15
  39.4 18.0 %collective-permute-start.3 = (f32[1,128,512]{2,1,0:T(8,128)S(1)}, f32[1,128,512]{2,1,0:T(8,128)S(1)}, u32[]{:S(2)}, u32[]{:S(2)}) collective-permute-start(f32[1,128,512]{2,1,0:T(8,128)S(1)} %get-tuple-element.15), channel_id=1, source_target_pairs={{1,0},{2,1},{3,2},{5,4},{6,5},{7,6},{9,8},{10,9},{11,10},{13,12},{... | collective-permute-start | bytes 786440 | tf_op jit(solution)/shard_map/ppermute | solution.py:17
  53.9 5.3 %collective-permute-start.6 = (f32[1,128,512]{2,1,0:T(8,128)S(1)}, f32[1,128,512]{2,1,0:T(8,128)S(1)}, u32[]{:S(2)}, u32[]{:S(2)}) collective-permute-start(f32[1,128,512]{2,1,0:T(8,128)S(1)} %get-tuple-element.16), channel_id=1, source_target_pairs={{0,1},{1,2},{2,3},{4,5},{5,6},{6,7},{8,9},{9,10},{10,11},{12,13},{... | collective-permute-start | bytes 786440 | tf_op jit(solution)/shard_map/ppermute | solution.py:15
  56.1 3.4 %collective-permute-start.7 = (f32[1,128,512]{2,1,0:T(8,128)S(1)}, f32[1,128,512]{2,1,0:T(8,128)S(1)}, u32[]{:S(2)}, u32[]{:S(2)}) collective-permute-start(f32[1,128,512]{2,1,0:T(8,128)S(1)} %get-tuple-element.17), channel_id=1, source_target_pairs={{1,0},{2,1},{3,2},{5,4},{6,5},{7,6},{9,8},{10,9},{11,10},{13,12},{... | collective-permute-start | bytes 786440 | tf_op jit(solution)/shard_map/ppermute | solution.py:17
  137.6 1.9 copy-start.5
  137.6 2.5 copy-start.6
  140.1 1.4 copy-start.15
  141.5 1.3 copy-start.9
  141.5 1.3 copy-start.11
  144.1 8.1 %copy-start.3 = (bf16[8,128,512]{2,1,0:T(8,128)(2,1)S(1)}, bf16[8,128,512]{2,1,0:T(8,128)(2,1)}, u32[]{:S(2)}) copy-start(bf16[8,128,512]{2,1,0:T(8,128)(2,1)} %fusion.36) | copy-start | bytes 3145732
  144.1 185.8 %all-reduce.9.cloned.1.call-start = ((), (), s32[]{:S(2)}) async-start(), calls=%async_computation.3 | async-start | bytes 6291456 | tf_op jit(solution)/shard_map/psum | solution.py:110
  145.2 5.1 %collective-permute-start.8 = (bf16[1,128,512]{2,1,0:T(8,128)(2,1)S(1)}, bf16[1,128,512]{2,1,0:T(8,128)(2,1)S(1)}, u32[]{:S(2)}, u32[]{:S(2)}) collective-permute-start(bf16[1,128,512]{2,1,0:T(8,128)(2,1)S(1)} %get-tuple-element.18), channel_id=1, source_target_pairs={{0,1},{1,2},{2,3},{4,5},{5,6},{6,7},{8,9},{9,10},{10,11},{12,13},{... | collective-permute-start | bytes 393224 | tf_op jit(solution)/shard_map/ppermute | solution.py:15
  148.9 3.2 collective-permute-start.9
  152.7 7.0 %copy-start.10 = (bf16[8,128,512]{2,1,0:T(8,128)(2,1)S(1)}, bf16[8,128,512]{2,1,0:T(8,128)(2,1)}, u32[]{:S(2)}) copy-start(bf16[8,128,512]{2,1,0:T(8,128)(2,1)} %copy-done.9) | copy-start | bytes 3145732
  152.8 7.0 %copy-start.12 = (bf16[8,128,512]{2,1,0:T(8,128)(2,1)S(1)}, bf16[8,128,512]{2,1,0:T(8,128)(2,1)}, u32[]{:S(2)}) copy-start(bf16[8,128,512]{2,1,0:T(8,128)(2,1)} %copy-done.11) | copy-start | bytes 3145732
  153.3 8.2 %collective-permute-start.10 = (f32[1,128,512]{2,1,0:T(8,128)S(1)}, f32[1,128,512]{2,1,0:T(8,128)S(1)}, u32[]{:S(2)}, u32[]{:S(2)}) collective-permute-start(f32[1,128,512]{2,1,0:T(8,128)S(1)} %get-tuple-element.12), channel_id=1, source_target_pairs={{0,1},{1,2},{2,3},{4,5},{5,6},{6,7},{8,9},{9,10},{10,11},{12,13},{... | collective-permute-start | bytes 786440 | tf_op jit(solution)/shard_map/ppermute | solution.py:15
  158.4 3.4 %collective-permute-start.11 = (f32[1,128,512]{2,1,0:T(8,128)S(1)}, f32[1,128,512]{2,1,0:T(8,128)S(1)}, u32[]{:S(2)}, u32[]{:S(2)}) collective-permute-start(f32[1,128,512]{2,1,0:T(8,128)S(1)} %get-tuple-element.13), channel_id=1, source_target_pairs={{1,0},{2,1},{3,2},{5,4},{6,5},{7,6},{9,8},{10,9},{11,10},{13,12},{... | collective-permute-start | bytes 786440 | tf_op jit(solution)/shard_map/ppermute | solution.py:17
  220.9 1.6 copy-start.4
  329.8 3.0 copy-start.8
Sparse Core Ops, SparseCore 0:
  13.2 41.4 all-gather.4
  56.9 34.7 all-gather.6
  144.2 39.1 all-gather.8
  225.9 103.8 all-reduce.8
where the time goes:
time: 341 us; the launch traced here: 340 us
  waiting for transfers between devices  129 us (38%)
  other arithmetic  108 us (32%)
  starting transfers between devices  35.3 us (10%)
  local copies, waits for them, and re-layouts  28.6 us (8%)
  between operations  14.2 us (4%)
  blocking collectives  13.1 us (4%)
  matrix products  11.9 us (3%)
    psum x1, waiting for transfers between devices, local(): lax.psum((grad_first, grad_second), ('dp', 'tile'))  100 us
    scatter-add x3, other arithmetic, propagate(): jax.ops.segment_sum(piece_values.reshape(-1, width).astype(jnp.float32),...  83.4 us
    ppermute x6, starting transfers between devices, extended(): lax.ppermute(tail, axis, [(i, (i + 1) % count) for i in range(ends)])  27.3 us
    all_gather x3, waiting for transfers between devices, propagate(): piece_values = lax.all_gather(scaled, 'tile', axis=0, tiled=True)  22.4 us
    gather x3, local copies, waits for them, and re-layouts, propagate(): jnp.take(cluster_mean, members.reshape(-1), axis=0).reshape(values.shape)  18.7 us
    all_gather x1, blocking collectives, propagate(): piece_members = lax.all_gather(members, 'tile', axis=0, tiled=True)  13.1 us
    convert_element_type x2, other arithmetic, propagate(): cluster_mean = (totals / sizes_float[:, None]).astype(jnp.bfloat16)  9.15 us
    ppermute x6, starting transfers between devices, extended(): lax.ppermute(head, axis, [((i + 1) % count, i) for i in range(ends)])  7.75 us
  transfers between devices with their start and end apart: 16, of which 7 were waited for; matrix products, arithmetic and copies ran while one was open for 13% of the time, Pallas kernels for 0%

commit v1 on v0

--- a/solution.py
+++ b/solution.py
@@ -45,7 +45,7 @@
     return row_part[:, None] * col_part[None, :]
 
 
-def propagate(values, members, member_sizes):
+def propagate(values, same, count):
     band_rows, grid_cols, width = values.shape
     bands = lax.axis_size("tile")
     row_start = lax.axis_index("tile") * band_rows
@@ -58,17 +58,11 @@
     spatial_mean = colbox(rowbox(padded.astype(jnp.float32))) / spread[..., None]
     widened = extended(spatial_mean, (("tile", 0),), 1)
     spatial = colbox(rowbox(widened))
-    clusters = member_sizes.shape[0]
-    sizes_float = member_sizes.astype(jnp.float32)
     piece_values = lax.all_gather(scaled, "tile", axis=0, tiled=True)
-    piece_members = lax.all_gather(members, "tile", axis=0, tiled=True)
-    totals = jax.ops.segment_sum(
-        piece_values.reshape(-1, width).astype(jnp.float32),
-        piece_members.reshape(-1),
-        num_segments=clusters,
+    total = jnp.dot(
+        same, piece_values.reshape(-1, width), preferred_element_type=jnp.float32
     )
-    cluster_mean = (totals / sizes_float[:, None]).astype(jnp.bfloat16)
-    picked = jnp.take(cluster_mean, members.reshape(-1), axis=0).reshape(values.shape)
+    picked = (total / count[:, None]).astype(jnp.bfloat16).reshape(values.shape)
     return (root[..., None] * (spatial + picked.astype(jnp.float32))).astype(jnp.bfloat16)
 
 
@@ -77,15 +71,17 @@
     band_rows, grid_cols, in_width = feats.shape
     hidden_width = weight_first.shape[1]
     out_width = weight_second.shape[1]
-    members = cluster_id[0]
-    member_sizes = cluster_size[0]
+    members = cluster_id[0].reshape(-1)
+    every = lax.all_gather(members, "tile", axis=0, tiled=True)
+    same = (members[:, None] == every[None, :]).astype(jnp.bfloat16)
+    count = jnp.take(cluster_size[0], members).astype(jnp.float32)
     flat_in = feats.reshape(-1, in_width)
     hidden_in = jnp.dot(flat_in, weight_first, preferred_element_type=jnp.float32).astype(
         jnp.bfloat16
     )
     hidden_grid = hidden_in.reshape(band_rows, grid_cols, hidden_width)
-    pre_act = propagate(hidden_grid, members, member_sizes)
-    back_second = propagate(cotangent[0], members, member_sizes)
+    pre_act = propagate(hidden_grid, same, count)
+    back_second = propagate(cotangent[0], same, count)
     pre_flat = pre_act.reshape(-1, hidden_width).astype(jnp.float32)
     sigma = jax.nn.sigmoid(pre_flat)
     activated = (pre_flat * sigma).astype(jnp.bfloat16)
@@ -98,7 +94,7 @@
     )
     grad_pre = (upstream * sigma * (1.0 + pre_flat * (1.0 - sigma))).astype(jnp.bfloat16)
     back_first = propagate(
-        grad_pre.reshape(band_rows, grid_cols, hidden_width), members, member_sizes
+        grad_pre.reshape(band_rows, grid_cols, hidden_width), same, count
     )
     first_flat = back_first.reshape(-1, hidden_width)
     grad_first = lax.dot_general(
@@ -107,8 +103,14 @@
     grad_feats = lax.dot_general(
         first_flat, weight_first, (((1,), (1,)), ((), ())), preferred_element_type=jnp.float32
     ).astype(jnp.bfloat16)
-    grad_first, grad_second = lax.psum((grad_first, grad_second), ("dp", "tile"))
-    return (grad_feats.reshape(1, band_rows, grid_cols, in_width), grad_first, grad_second)
+    grad_first, grad_second = lax.psum(
+        (grad_first.astype(jnp.bfloat16), grad_second.astype(jnp.bfloat16)), ("dp", "tile")
+    )
+    return (
+        grad_feats.reshape(1, band_rows, grid_cols, in_width),
+        grad_first.astype(jnp.float32),
+        grad_second.astype(jnp.float32),
+    )
 
 
 def solution(mesh):

time: 341 us -> 262 us (0.77)
  other arithmetic: 108 us -> 20.3 us
  matrix products: 11.9 us -> 32.1 us
  local copies, waits for them, and re-layouts: 28.6 us -> 14.8 us
  waiting for transfers between devices: 129 us -> 141 us
  blocking collectives: 13.1 us -> 7.36 us
  starting transfers between devices: 35.3 us -> 30.9 us
    scatter-add x3 -> x0, other arithmetic: 83.4 us -> none  [propagate(): jax.ops.segment_sum(piece_values.reshape(-1, width).astype(jnp.float32),...]
    dot_general x0 -> x3, matrix products: none -> 20.6 us  [propagate(): jnp.dot(same, piece_values.reshape(-1, width), preferred_element_type=jnp...]
    all_gather x3, waiting for transfers between devices: 22.4 us -> 41.8 us  [propagate(): piece_values = lax.all_gather(scaled, 'tile', axis=0, tiled=True)]
    gather x3 -> x1, local copies, waits for them, and re-layouts: 18.7 us -> 6.15 us  [local(): count = jnp.take(cluster_size[0], members).astype(jnp.float32)]
    psum x1, waiting for transfers between devices: 100 us -> 92.1 us  [local(): lax.psum((grad_first.astype(jnp.bfloat16), grad_second.astype(jnp.bfloat1...]
    convert_element_type x3 -> x2, other arithmetic: 9.16 us -> 1.11 us  [the longest x1 1.1 us: local(): grad_second.astype(jnp.float32)]
    all_gather x1, blocking collectives: 13.1 us -> 7.36 us  [local(): every = lax.all_gather(members, 'tile', axis=0, tiled=True)]
    ppermute x6, starting transfers between devices: 27.3 us -> 22.6 us  [extended(): lax.ppermute(tail, axis, [(i, (i + 1) % count) for i in range(ends)])]
  transfers between devices with their start and end apart: 16 -> 16, of which waited for: 7 -> 9; matrix products, arithmetic and copies ran while one was open for 13% -> 11% of each run, Pallas kernels for 0% -> 0%
where the time goes in v1:
time: 262 us; the launch traced here: 261 us
  waiting for transfers between devices  141 us (54%)
  matrix products  32.1 us (12%)
  starting transfers between devices  30.9 us (12%)
  other arithmetic  20.3 us (8%)
  local copies, waits for them, and re-layouts  14.8 us (6%)
  between operations  14.2 us (5%)
  blocking collectives  7.36 us (3%)
    psum x1, waiting for transfers between devices, local(): lax.psum((grad_first.astype(jnp.bfloat16), grad_second.astype(jnp.bfloat1...  92.1 us
    all_gather x3, waiting for transfers between devices, propagate(): piece_values = lax.all_gather(scaled, 'tile', axis=0, tiled=True)  41.8 us
    ppermute x6, starting transfers between devices, extended(): lax.ppermute(tail, axis, [(i, (i + 1) % count) for i in range(ends)])  22.6 us
    dot_general x3, matrix products, propagate(): jnp.dot(same, piece_values.reshape(-1, width), preferred_element_type=jnp...  20.6 us
    add x6, other arithmetic, rowbox(): return values[:-2] + values[1:-1] + values[2:]  9.47 us
    ppermute x6, starting transfers between devices, extended(): lax.ppermute(head, axis, [((i + 1) % count, i) for i in range(ends)])  8.15 us
    ppermute x6, waiting for transfers between devices, extended(): lax.ppermute(head, axis, [((i + 1) % count, i) for i in range(ends)])  7.51 us
    all_gather x1, blocking collectives, local(): every = lax.all_gather(members, 'tile', axis=0, tiled=True)  7.36 us
  transfers between devices with their start and end apart: 16, of which 9 were waited for; matrix products, arithmetic and copies ran while one was open for 11% of the time, Pallas kernels for 0%

profile of v1, /device:TPU:0, one launch (start us, length us, event | category | flops | bytes accessed | tf_op | source)
XLA Modules:
  0.0 261.1 jit_solution(1679611667894408712)
XLA Ops:
  7.2 0.0 all-gather.4.cloned.1.call-start
  7.3 0.1 broadcast_multiply_fusion
  7.3 2.6 %fusion.44 = bf16[8,128,512]{2,1,0:T(8,128)(2,1)} fusion(bf16[1,8,128,512]{3,2,1,0:T(8,128)(2,1)} %param.7, f32[8,128]{1,0:T(8,128)S(1)} %get-tuple-element.29), kind=kLoop, calls=%fused_computation.72 | loop fusion | flops 1572864 | bytes 2101248 | tf_op jit(solution)/shard_map/convert_element_type | solution.py:56
  10.0 0.0 all-gather.4.cloned.1.call-update
  10.0 0.0 all-gather.6.cloned.1.call-start
  10.0 1.0 fusion.73
  11.0 2.4 collective-permute-start
  13.4 1.3 collective-permute-start.1
  14.7 2.6 convolution_convert_fusion.2
  17.3 1.4 collective-permute-done.1
  18.7 0.2 maximum_convert_fusion
  18.9 0.4 slice_add_fusion.4
  19.4 0.5 fusion.14
  19.9 1.3 copy-done.5
  21.2 0.8 fusion.70
  22.1 5.5 %collective-permute-start.2 = (f32[1,128,512]{2,1,0:T(8,128)}, f32[1,128,512]{2,1,0:T(8,128)S(1)}, u32[]{:S(2)}, u32[]{:S(2)}) collective-permute-start(f32[1,128,512]{2,1,0:T(8,128)} %get-tuple-element.16), channel_id=1, source_target_pairs={{0,1},{1,2},{2,3},{4,5},{5,6},{6,7},{8,9},{9,10},{10,11},{12,13},{... | collective-permute-start | bytes 786440 | tf_op jit(solution)/shard_map/ppermute | solution.py:15
  27.5 1.3 collective-permute-start.3
  28.8 6.2 %gather_fusion = s32[1024]{0:T(1024)S(1)} fusion(s32[2048]{0:T(1024)S(1)} %bitcast.62, s32[1024]{0:T(1024)S(1)} %broadcast_clamp_fusion), kind=kCustom, calls=%fused_computation | custom fusion | bytes 12288 | tf_op jit(solution)/shard_map/jit(_take)/gather | solution.py:77
  35.0 7.4 %all_gather.12 = s32[4096]{0:T(1024)S(1)} all-gather(s32[1024]{0:T(1024)S(1)} %bitcast.72), channel_id=1, replica_groups=mesh['groups'=2,'dp'=4,'tile'=4] {'tile'}, dimensions={0}, use_global_device_ids=true | all-gather | bytes 20480 | tf_op jit(solution)/shard_map/all_gather | solution.py:75
  42.4 4.9 %fusion.40 = f32[8,128,512]{2,1,0:T(8,128)} fusion(f32[1,128,512]{2,1,0:T(8,128)} %collective-permute-done.3, f32[8,128,512]{2,1,0:T(8,128)} %copy-done.5, f32[1,128,512]{2,1,0:T(8,128)S(1)} %collective-permute-done.2), kind=kLoop, calls=%fused_computation.62 | loop fusion | flops 2097152 | bytes 4718592 | tf_op jit(solution)/shard_map/add | solution.py:25
  47.3 2.9 %all-gather.4.cloned.1.call-done = bf16[32,128,512]{2,1,0:T(8,128)(2,1)} async-done(((bf16[8,128,512]{2,1,0:T(8,128)(2,1)}), bf16[32,128,512]{2,1,0:T(8,128)(2,1)}) %all-gather.4.cloned.1.call-update) | async-done | bytes 4194320 | tf_op jit(solution)/shard_map/all_gather | solution.py:61
  50.3 6.9 %divide_convert_fusion.2 = bf16[1024,512]{1,0:T(8,128)(2,1)S(1)} fusion(bf16[4096,512]{1,0:T(8,128)(2,1)} %bitcast.77, s32[4096]{0:T(1024)S(1)} %all_gather.12, s32[1024]{0:T(1024)S(1)} %bitcast.73, f32[1024]{0:T(1024)S(1)} %select_convert_fusion), kind=kOutput, calls=%fused_computation.89 | convolution fusion | flops 4300210176 | bytes 5267456 | tf_op jit(solution)/shard_map/dot_general | solution.py:62
  57.1 2.2 fusion.19
  59.3 0.0 all-gather.6.cloned.1.call-update
  59.3 0.0 all-gather.8.cloned.1.call-start
  59.4 1.1 fusion.74
  60.5 2.2 collective-permute-start.4
  62.6 1.3 collective-permute-start.5
  63.9 1.9 collective-permute-done.5
  65.9 0.2 maximum_convert_fusion.1
  66.1 0.3 slice_add_fusion.2
  66.4 0.5 fusion.22
  67.0 5.1 %collective-permute-start.6 = (f32[1,128,512]{2,1,0:T(8,128)S(1)}, f32[1,128,512]{2,1,0:T(8,128)S(1)}, u32[]{:S(2)}, u32[]{:S(2)}) collective-permute-start(f32[1,128,512]{2,1,0:T(8,128)S(1)} %get-tuple-element.18), channel_id=1, source_target_pairs={{0,1},{1,2},{2,3},{4,5},{5,6},{6,7},{8,9},{9,10},{10,11},{12,13},{... | collective-permute-start | bytes 786440 | tf_op jit(solution)/shard_map/ppermute | solution.py:15
  72.1 1.5 collective-permute-start.7
  73.6 1.9 collective-permute-done.7
  75.6 1.7 fusion.38
  77.3 19.5 %all-gather.6.cloned.1.call-done = bf16[32,128,512]{2,1,0:T(8,128)(2,1)} async-done(((bf16[8,128,512]{2,1,0:T(8,128)(2,1)}), bf16[32,128,512]{2,1,0:T(8,128)(2,1)}) %all-gather.6.cloned.1.call-update) | async-done | bytes 4194320 | tf_op jit(solution)/shard_map/all_gather | solution.py:61
  96.8 6.9 %divide_convert_fusion.1 = bf16[1024,512]{1,0:T(8,128)(2,1)S(1)} fusion(bf16[4096,512]{1,0:T(8,128)(2,1)} %bitcast.79, s32[4096]{0:T(1024)S(1)} %all_gather.12, s32[1024]{0:T(1024)S(1)} %bitcast.74, f32[1024]{0:T(1024)S(1)} %select_convert_fusion), kind=kOutput, calls=%fused_computation.88 | convolution fusion | flops 4300210176 | bytes 5267456 | tf_op jit(solution)/shard_map/dot_general | solution.py:62
  103.7 0.7 fusion.27
  104.4 0.5 copy-done.11
  104.9 0.1 copy-done.15
  105.0 1.2 fusion.54
  106.3 1.3 fusion.42
  107.6 0.0 all-reduce.9.cloned.1.call-start
  107.6 1.1 fusion.72
  108.7 2.2 collective-permute-start.8
  110.9 1.3 collective-permute-start.9
  112.2 1.9 collective-permute-done.9
  114.1 0.2 maximum_convert_fusion.2
  114.3 0.3 slice_add_fusion
  114.7 0.5 fusion.30
  115.3 5.3 %collective-permute-start.10 = (f32[1,128,512]{2,1,0:T(8,128)S(1)}, f32[1,128,512]{2,1,0:T(8,128)S(1)}, u32[]{:S(2)}, u32[]{:S(2)}) collective-permute-start(f32[1,128,512]{2,1,0:T(8,128)S(1)} %get-tuple-element.14), channel_id=1, source_target_pairs={{0,1},{1,2},{2,3},{4,5},{5,6},{6,7},{8,9},{9,10},{10,11},{12,13},{... | collective-permute-start | bytes 786440 | tf_op jit(solution)/shard_map/ppermute | solution.py:15
  120.5 1.5 collective-permute-start.11
  122.1 1.6 fusion.62
  123.7 0.3 collective-permute-done.11
  124.0 1.7 fusion.36
  125.7 19.3 %all-gather.8.cloned.1.call-done = bf16[32,128,512]{2,1,0:T(8,128)(2,1)} async-done(((bf16[8,128,512]{2,1,0:T(8,128)(2,1)}), bf16[32,128,512]{2,1,0:T(8,128)(2,1)}) %all-gather.8.cloned.1.call-update) | async-done | bytes 4194320 | tf_op jit(solution)/shard_map/all_gather | solution.py:61
  145.0 6.9 %divide_convert_fusion = bf16[1024,512]{1,0:T(8,128)(2,1)S(1)} fusion(bf16[4096,512]{1,0:T(8,128)(2,1)} %bitcast.78, s32[4096]{0:T(1024)S(1)} %all_gather.12, s32[1024]{0:T(1024)S(1)} %bitcast.75, f32[1024]{0:T(1024)S(1)} %select_convert_fusion), kind=kOutput, calls=%fused_computation.87 | convolution fusion | flops 4300210176 | bytes 5267456 | tf_op jit(solution)/shard_map/dot_general | solution.py:62
  151.9 0.7 fusion.35
  152.6 2.2 fusion.61
  154.9 3.8 %convolution_convert_fusion = bf16[1024,1024]{1,0:T(8,128)(2,1)} fusion(bf16[1024,512]{1,0:T(8,128)(2,1)S(1)} %bitcast.64, bf16[1024,512]{1,0:T(8,128)(2,1)} %param.8), kind=kOutput, calls=%fused_computation.90 | convolution fusion | flops 1074790400 | bytes 4194304 | tf_op jit(solution)/shard_map/dot_general | solution.py:103
  158.7 92.1 %all-reduce.9.cloned.1.call-done = (bf16[1024,512]{0,1:T(8,128)(2,1)}, bf16[512,512]{1,0:T(8,128)(2,1)}) async-done(((bf16[1024,512]{0,1:T(8,128)(2,1)}, bf16[512,512]{1,0:T(8,128)(2,1)}), (bf16[1024,512]{0,1:T(8,128)(2,1)}, bf16[512,512]{1,0:T(8,128)(2,1)})) %all-reduce.9.cloned.1.call-update) | async-done | bytes 1572880 | tf_op jit(solution)/shard_map/psum | solution.py:106
  250.8 2.6 %copy.14 = f32[1024,512]{1,0:T(8,128)} copy(bf16[1024,512]{0,1:T(8,128)(2,1)} %get-tuple-element.12) | data formatting | bytes 3145728
  253.5 1.1 convert_element_type.200
  (45 shorter events, 0.2 us)
Async XLA Ops:
  7.2 7.5 %copy-start = (bf16[1,8,128,1024]{3,2,1,0:T(8,128)(2,1)S(1)}, bf16[1,8,128,1024]{3,2,1,0:T(8,128)(2,1)}, u32[]{:S(2)}) copy-start(bf16[1,8,128,1024]{3,2,1,0:T(8,128)(2,1)} %param.6) | copy-start | bytes 6291460
  7.2 43.1 %all-gather.4.cloned.1.call-start = ((), (), s32[]{:S(2)}) async-start(), calls=%async_computation | async-start | bytes 5242880 | tf_op jit(solution)/shard_map/all_gather | solution.py:61
  10.0 86.8 %all-gather.6.cloned.1.call-start = ((), (), s32[]{:S(2)}) async-start(), calls=%async_computation.1 | async-start | bytes 5242880 | tf_op jit(solution)/shard_map/all_gather | solution.py:61
  11.0 6.3 %collective-permute-start = (bf16[1,128,512]{2,1,0:T(8,128)(2,1)S(1)}, bf16[1,128,512]{2,1,0:T(8,128)(2,1)S(1)}, u32[]{:S(2)}, u32[]{:S(2)}) collective-permute-start(bf16[1,128,512]{2,1,0:T(8,128)(2,1)S(1)} %get-tuple-element.22), channel_id=1, source_target_pairs={{0,1},{1,2},{2,3},{4,5},{5,6},{6,7},{8,9},{9,10},{10,11},{12,13},{... | collective-permute-start | bytes 393224 | tf_op jit(solution)/shard_map/ppermute | solution.py:15
  13.4 5.3 %collective-permute-start.1 = (bf16[1,128,512]{2,1,0:T(8,128)(2,1)S(1)}, bf16[1,128,512]{2,1,0:T(8,128)(2,1)S(1)}, u32[]{:S(2)}, u32[]{:S(2)}) collective-permute-start(bf16[1,128,512]{2,1,0:T(8,128)(2,1)S(1)} %get-tuple-element.23), channel_id=1, source_target_pairs={{1,0},{2,1},{3,2},{5,4},{6,5},{7,6},{9,8},{10,9},{11,10},{13,12},{... | collective-permute-start | bytes 393224 | tf_op jit(solution)/shard_map/ppermute | solution.py:17
  14.7 2.6 copy-start.14
  14.7 4.0 %copy-start.2 = (bf16[8,128,512]{2,1,0:T(8,128)(2,1)S(1)}, bf16[8,128,512]{2,1,0:T(8,128)(2,1)}, u32[]{:S(2)}) copy-start(bf16[8,128,512]{2,1,0:T(8,128)(2,1)} %fusion.44) | copy-start | bytes 3145732
  19.4 9.5 %copy-start.1 = (s32[1,2048]{1,0:T(1,128)S(1)}, s32[1,2048]{1,0:T(1,128)}, u32[]{:S(2)}) copy-start(s32[1,2048]{1,0:T(1,128)} %param.11) | copy-start | bytes 24580
  19.9 1.3 copy-start.5
  22.1 20.3 %collective-permute-start.2 = (f32[1,128,512]{2,1,0:T(8,128)}, f32[1,128,512]{2,1,0:T(8,128)S(1)}, u32[]{:S(2)}, u32[]{:S(2)}) collective-permute-start(f32[1,128,512]{2,1,0:T(8,128)} %get-tuple-element.16), channel_id=1, source_target_pairs={{0,1},{1,2},{2,3},{4,5},{5,6},{6,7},{8,9},{9,10},{10,11},{12,13},{... | collective-permute-start | bytes 786440 | tf_op jit(solution)/shard_map/ppermute | solution.py:15
  27.5 14.9 %collective-permute-start.3 = (f32[1,128,512]{2,1,0:T(8,128)}, f32[1,128,512]{2,1,0:T(8,128)}, u32[]{:S(2)}, u32[]{:S(2)}) collective-permute-start(f32[1,128,512]{2,1,0:T(8,128)} %get-tuple-element.17), channel_id=1, source_target_pairs={{1,0},{2,1},{3,2},{5,4},{6,5},{7,6},{9,8},{10,9},{11,10},{13,12},{... | collective-permute-start | bytes 786440 | tf_op jit(solution)/shard_map/ppermute | solution.py:17
  50.3 6.9 %copy-start.8 = (f32[8,128,512]{2,1,0:T(8,128)S(1)}, f32[8,128,512]{2,1,0:T(8,128)}, u32[]{:S(2)}) copy-start(f32[8,128,512]{2,1,0:T(8,128)} %fusion.40) | copy-start | bytes 6291460
  59.3 6.6 %copy-start.4 = (bf16[8,128,512]{2,1,0:T(8,128)(2,1)S(1)}, bf16[8,128,512]{2,1,0:T(8,128)(2,1)}, u32[]{:S(2)}) copy-start(bf16[8,128,512]{2,1,0:T(8,128)(2,1)} %get-tuple-element.27) | copy-start | bytes 3145732
  59.3 85.7 %all-gather.8.cloned.1.call-start = ((), (), s32[]{:S(2)}) async-start(), calls=%async_computation.2 | async-start | bytes 5242880 | tf_op jit(solution)/shard_map/all_gather | solution.py:61
  60.5 3.5 %collective-permute-start.4 = (bf16[1,128,512]{2,1,0:T(8,128)(2,1)S(1)}, bf16[1,128,512]{2,1,0:T(8,128)(2,1)S(1)}, u32[]{:S(2)}, u32[]{:S(2)}) collective-permute-start(bf16[1,128,512]{2,1,0:T(8,128)(2,1)S(1)} %get-tuple-element.24), channel_id=1, source_target_pairs={{0,1},{1,2},{2,3},{4,5},{5,6},{6,7},{8,9},{9,10},{10,11},{12,13},{... | collective-permute-start | bytes 393224 | tf_op jit(solution)/shard_map/ppermute | solution.py:15
  62.6 3.2 %collective-permute-start.5 = (bf16[1,128,512]{2,1,0:T(8,128)(2,1)S(1)}, bf16[1,128,512]{2,1,0:T(8,128)(2,1)S(1)}, u32[]{:S(2)}, u32[]{:S(2)}) collective-permute-start(bf16[1,128,512]{2,1,0:T(8,128)(2,1)S(1)} %get-tuple-element.25), channel_id=1, source_target_pairs={{1,0},{2,1},{3,2},{5,4},{6,5},{7,6},{9,8},{10,9},{11,10},{13,12},{... | collective-permute-start | bytes 393224 | tf_op jit(solution)/shard_map/ppermute | solution.py:17
  67.0 6.6 %collective-permute-start.6 = (f32[1,128,512]{2,1,0:T(8,128)S(1)}, f32[1,128,512]{2,1,0:T(8,128)S(1)}, u32[]{:S(2)}, u32[]{:S(2)}) collective-permute-start(f32[1,128,512]{2,1,0:T(8,128)S(1)} %get-tuple-element.18), channel_id=1, source_target_pairs={{0,1},{1,2},{2,3},{4,5},{5,6},{6,7},{8,9},{9,10},{10,11},{12,13},{... | collective-permute-start | bytes 786440 | tf_op jit(solution)/shard_map/ppermute | solution.py:15
  72.1 3.4 %collective-permute-start.7 = (f32[1,128,512]{2,1,0:T(8,128)S(1)}, f32[1,128,512]{2,1,0:T(8,128)S(1)}, u32[]{:S(2)}, u32[]{:S(2)}) collective-permute-start(f32[1,128,512]{2,1,0:T(8,128)S(1)} %get-tuple-element.19), channel_id=1, source_target_pairs={{1,0},{2,1},{3,2},{5,4},{6,5},{7,6},{9,8},{10,9},{11,10},{13,12},{... | collective-permute-start | bytes 786440 | tf_op jit(solution)/shard_map/ppermute | solution.py:17
  96.8 6.9 %copy-start.7 = (f32[8,128,512]{2,1,0:T(8,128)S(1)}, f32[8,128,512]{2,1,0:T(8,128)}, u32[]{:S(2)}) copy-start(f32[8,128,512]{2,1,0:T(8,128)} %fusion.38) | copy-start | bytes 6291460
  103.7 1.2 copy-start.11
  103.7 1.3 copy-start.15
  104.4 1.9 copy-start.9
  107.6 6.6 %copy-start.3 = (bf16[8,128,512]{2,1,0:T(8,128)(2,1)S(1)}, bf16[8,128,512]{2,1,0:T(8,128)(2,1)}, u32[]{:S(2)}) copy-start(bf16[8,128,512]{2,1,0:T(8,128)(2,1)} %fusion.42) | copy-start | bytes 3145732
  107.6 143.2 %all-reduce.9.cloned.1.call-start = ((), (), s32[]{:S(2)}) async-start(), calls=%async_computation.3 | async-start | bytes 3145728 | tf_op jit(solution)/shard_map/psum | solution.py:106
  108.7 3.5 %collective-permute-start.8 = (bf16[1,128,512]{2,1,0:T(8,128)(2,1)S(1)}, bf16[1,128,512]{2,1,0:T(8,128)(2,1)S(1)}, u32[]{:S(2)}, u32[]{:S(2)}) collective-permute-start(bf16[1,128,512]{2,1,0:T(8,128)(2,1)S(1)} %get-tuple-element.20), channel_id=1, source_target_pairs={{0,1},{1,2},{2,3},{4,5},{5,6},{6,7},{8,9},{9,10},{10,11},{12,13},{... | collective-permute-start | bytes 393224 | tf_op jit(solution)/shard_map/ppermute | solution.py:15
  110.9 3.2 %collective-permute-start.9 = (bf16[1,128,512]{2,1,0:T(8,128)(2,1)S(1)}, bf16[1,128,512]{2,1,0:T(8,128)(2,1)S(1)}, u32[]{:S(2)}, u32[]{:S(2)}) collective-permute-start(bf16[1,128,512]{2,1,0:T(8,128)(2,1)S(1)} %get-tuple-element.21), channel_id=1, source_target_pairs={{1,0},{2,1},{3,2},{5,4},{6,5},{7,6},{9,8},{10,9},{11,10},{13,12},{... | collective-permute-start | bytes 393224 | tf_op jit(solution)/shard_map/ppermute | solution.py:17
  114.7 7.4 %copy-start.10 = (bf16[8,128,512]{2,1,0:T(8,128)(2,1)S(1)}, bf16[8,128,512]{2,1,0:T(8,128)(2,1)}, u32[]{:S(2)}) copy-start(bf16[8,128,512]{2,1,0:T(8,128)(2,1)} %copy-done.9) | copy-start | bytes 3145732
  114.7 7.4 %copy-start.12 = (bf16[8,128,512]{2,1,0:T(8,128)(2,1)S(1)}, bf16[8,128,512]{2,1,0:T(8,128)(2,1)}, u32[]{:S(2)}) copy-start(bf16[8,128,512]{2,1,0:T(8,128)(2,1)} %get-tuple-element.26) | copy-start | bytes 3145732
  115.3 8.4 %collective-permute-start.10 = (f32[1,128,512]{2,1,0:T(8,128)S(1)}, f32[1,128,512]{2,1,0:T(8,128)S(1)}, u32[]{:S(2)}, u32[]{:S(2)}) collective-permute-start(f32[1,128,512]{2,1,0:T(8,128)S(1)} %get-tuple-element.14), channel_id=1, source_target_pairs={{0,1},{1,2},{2,3},{4,5},{5,6},{6,7},{8,9},{9,10},{10,11},{12,13},{... | collective-permute-start | bytes 786440 | tf_op jit(solution)/shard_map/ppermute | solution.py:15
  120.5 3.4 %collective-permute-start.11 = (f32[1,128,512]{2,1,0:T(8,128)S(1)}, f32[1,128,512]{2,1,0:T(8,128)S(1)}, u32[]{:S(2)}, u32[]{:S(2)}) collective-permute-start(f32[1,128,512]{2,1,0:T(8,128)S(1)} %get-tuple-element.15), channel_id=1, source_target_pairs={{1,0},{2,1},{3,2},{5,4},{6,5},{7,6},{9,8},{10,9},{11,10},{13,12},{... | collective-permute-start | bytes 786440 | tf_op jit(solution)/shard_map/ppermute | solution.py:17
  145.0 6.9 %copy-start.6 = (f32[8,128,512]{2,1,0:T(8,128)S(1)}, f32[8,128,512]{2,1,0:T(8,128)}, u32[]{:S(2)}) copy-start(f32[8,128,512]{2,1,0:T(8,128)} %fusion.36) | copy-start | bytes 6291460
  250.8 2.6 %copy-start.13 = (bf16[512,512]{1,0:T(8,128)(2,1)S(1)}, bf16[512,512]{1,0:T(8,128)(2,1)}, u32[]{:S(2)}) copy-start(bf16[512,512]{1,0:T(8,128)(2,1)} %get-tuple-element.13) | copy-start | bytes 1572868
Sparse Core Ops, SparseCore 0:
  10.1 40.0 all-gather.3
  59.5 37.2 all-gather.5
  107.7 37.2 all-gather.7
  155.0 95.7 all-reduce.8

commit v2 on v1

--- a/solution.py
+++ b/solution.py
@@ -1,6 +1,8 @@
 import jax
 import jax.numpy as jnp
 from jax import lax
+from jax.experimental import pallas as pl
+from jax.experimental.pallas import tpu as pltpu
 from jax.sharding import PartitionSpec as P
 
 
@@ -113,6 +115,355 @@
     )
 
 
+F32, BF16 = jnp.float32, jnp.bfloat16
+MESH = pl.DeviceIdType.MESH
+NT = (((1,), (1,)), ((), ()))
+TN = (((0,), (0,)), ((), ()))
+
+
+def dot(a, b, dims=(((1,), (0,)), ((), ()))):
+    return lax.dot_general(a, b, dims, preferred_element_type=F32)
+
+
+def lanes(table, width):
+    return jnp.concatenate([table] * (width // 128), axis=1)
+
+
+def kernel(
+    x_ref, c_ref, w1_ref, w2_ref, id_ref, out_ref, gf_ref, gs_ref,
+    ids, same, rcnt, sc, sh, sg, hs, back, act, tot, ups, first, fsend,
+    gf, gs, gfb, gsb, gfr, gsr, gfx, gfxr, gfz, gsz, gfzr, gszr, sends, recvs,
+):
+    t = lax.axis_index("tile")
+    z = lax.axis_index("dp")
+    x, c = t // 2, t % 2
+    other = (1 - x) * 2 + c
+    core = x * 2 + (1 - c)
+    diag = (1 - x) * 2 + (1 - c)
+    zs = [lax.rem(z + d, 4) for d in (1, 2, 3)]
+    barrier = pltpu.get_barrier_semaphore()
+    for peer in (other, core, diag):
+        pl.semaphore_signal(barrier, inc=1, device_id={"tile": peer}, device_id_type=MESH)
+    for peer in zs:
+        pl.semaphore_signal(barrier, inc=1, device_id={"dp": peer}, device_id_type=MESH)
+
+    used = [0]
+    pending = []
+
+    def send(src, dst, where, track=True):
+        k = used[0]
+        used[0] += 1
+        copy = pltpu.make_async_remote_copy(
+            src_ref=src, dst_ref=dst, send_sem=sends.at[k], recv_sem=recvs.at[k],
+            device_id=where, device_id_type=MESH,
+        )
+        copy.start()
+        if track:
+            pending.append(copy)
+        return copy
+
+    def flush():
+        for copy in pending:
+            copy.wait_send()
+        pending.clear()
+
+    col = lax.broadcasted_iota(jnp.int32, (128, 128), 0)
+    cp = jnp.where((col == 0) | (col == 127), 2.0, 3.0).astype(F32)
+
+    def root_of(i):
+        rp = jnp.where((i == 0) | (i == 31), 2.0, 3.0)
+        return 1.0 / jnp.sqrt(rp * cp + 1.0)
+
+    def q_of(i):
+        inside = (i >= 0) & (i <= 31)
+        return jnp.where(inside, jnp.where((i == 0) | (i == 31), 0.5, 1.0 / 3.0), 0.0)
+
+    def grid_rows(ref, i, count=1):
+        return ref.at[pl.ds(pl.multiple_of((i + 2) * 128, 128), 128 * count), :]
+
+    ids[pl.ds(pl.multiple_of(t * 8, 8), 8), :] = id_ref[...]
+
+    def scale_c(r, _):
+        i = t * 8 + r
+        v = c_ref[pl.ds(pl.multiple_of(r * 128, 128), 128), :].astype(F32)
+        sc[pl.ds(pl.multiple_of((i + 2) * 128, 128), 128), :] = (
+            v * lanes(root_of(i), 512)
+        ).astype(BF16)
+        return 0
+
+    lax.fori_loop(0, 8, scale_c, 0)
+    for ref in (sc, sh, sg):
+        ref[0:256, :] = jnp.zeros((256, ref.shape[1]), BF16)
+        ref[4352:4608, :] = jnp.zeros((256, ref.shape[1]), BF16)
+
+    pl.semaphore_wait(barrier, 6)
+    mine = ids.at[pl.ds(pl.multiple_of(t * 8, 8), 8), :]
+    id_copies = [send(mine, mine, {"tile": p}) for p in (other, core, diag)]
+    cx = []
+    for part in range(4):
+        block = grid_rows(sc, t * 8 + part * 2, 2)
+        cx.append(send(block, block, {"tile": other}, False))
+    own = grid_rows(sc, t * 8, 8)
+    c_core = send(own, own, {"tile": core})
+
+    def hidden(g, _):
+        rows = pl.ds(pl.multiple_of(g * 256, 256), 256)
+        for j in range(2):
+            hv = dot(x_ref[rows, :], w1_ref[:, j * 256 : j * 256 + 256]).astype(BF16)
+            for k in range(2):
+                i = t * 8 + g * 2 + k
+                s = hv[k * 128 : k * 128 + 128].astype(F32) * lanes(root_of(i), 256)
+                hs[j, pl.ds(pl.multiple_of(g * 256 + k * 128, 128), 128), :] = s.astype(BF16)
+        return 0
+
+    lax.fori_loop(0, 4, hidden, 0)
+    rows_h = grid_rows(sh, t * 8, 8)
+    h_core = send(hs.at[x], rows_h, {"tile": core})
+    sh[pl.ds(pl.multiple_of((t * 8 + 2) * 128, 128), 1024), :] = hs[x]
+
+    for copy in id_copies:
+        copy.wait_recv()
+
+    def build(rr, _):
+        band = (rr // 8) * 2 + c
+        row = ids[pl.ds(band * 8 + rr % 8, 1), :].astype(F32)
+        tall = jnp.transpose(jnp.broadcast_to(row, (128, 128)))
+        acc = jnp.zeros((128, 128), F32)
+        dst = pl.ds(pl.multiple_of(rr * 128, 128), 128)
+        for k in range(32):
+            v = jnp.where(tall == ids[k : k + 1, :].astype(F32), 1.0, 0.0)
+            acc = acc + v
+            same[dst, k * 128 : k * 128 + 128] = v.astype(BF16)
+        rcnt[dst, :] = jnp.broadcast_to(1.0 / jnp.sum(acc, axis=1, keepdims=True), (128, 128))
+        return 0
+
+    lax.fori_loop(0, 16, build, 0)
+
+    def prop(src, width, xb, emit, before=None):
+        def group(g, _):
+            rows = pl.ds(pl.multiple_of(xb * 1024 + g * 512, 512), 512)
+            tot[:, :width] = dot(same[rows, :], src[256:4352, :])
+            if before is not None:
+                before(rows)
+
+            def one(r, _):
+                lr = g * 4 + r
+                i = (xb * 2 + c) * 8 + lr
+                qs = [q_of(i - 1), q_of(i), q_of(i + 1)]
+                taps = [qs[0], qs[0] + qs[1], qs[0] + qs[1] + qs[2], qs[1] + qs[2], qs[2]]
+                local = pl.ds(pl.multiple_of(r * 128, 128), 128)
+                at = pl.ds(pl.multiple_of(xb * 1024 + lr * 128, 128), 128)
+                root = root_of(i)
+                for w in range(0, width, 256):
+                    ch = slice(w, w + 256)
+                    v = jnp.zeros((128, 256), F32)
+                    for k in range(5):
+                        rowk = src[pl.ds(pl.multiple_of((i + k) * 128, 128), 128), ch]
+                        v = v + taps[k] * rowk.astype(F32)
+                    colw = lanes(col, 256)
+
+                    def colbox(u):
+                        up = jnp.where(colw == 0, 0.0, pltpu.roll(u, 1, 0))
+                        down = jnp.where(colw == 127, 0.0, pltpu.roll(u, 127, 0))
+                        return u + up + down
+
+                    v = colbox(colbox(v) * lanes(1.0 / cp, 256))
+                    mean = (tot[local, ch] * lanes(rcnt[at, :], 256)).astype(BF16)
+                    emit(lr, i, at, local, ch, root, lanes(root, 256) * (v + mean.astype(F32)))
+                return 0
+
+            lax.fori_loop(0, 4, one, 0)
+            return 0
+
+        lax.fori_loop(0, 2, group, 0)
+
+    fw = []
+    for part in range(4):
+        cx[part].wait_recv()
+        block = grid_rows(sc, other * 8 + part * 2, 2)
+        fw.append(send(block, block, {"tile": core}))
+    for part in range(4):
+        cx[part].wait_send()
+    h_x = send(hs.at[1 - x], rows_h, {"tile": other})
+    c_core.wait_recv()
+    for copy in fw:
+        copy.wait_recv()
+
+    def emit_c(lr, i, at, local, ch, root, value):
+        back[at, ch] = value.astype(BF16)
+
+    prop(sc, 512, 0, emit_c)
+    prop(sc, 512, 1, emit_c)
+
+    h_x.wait_recv()
+    block = grid_rows(sh, other * 8, 8)
+    h_fw = send(block, block, {"tile": core})
+    h_core.wait_recv()
+    h_fw.wait_recv()
+
+    def before_h(rows):
+        half = w2_ref[pl.ds(pl.multiple_of(x * 256, 256), 256), :]
+        ups[...] = dot(back[rows, :], half, NT)
+
+    def emit_h(lr, i, at, local, ch, root, value):
+        p = value.astype(BF16).astype(F32)
+        sig = 1.0 / (1.0 + jnp.exp(-p))
+        act[at, :] = (p * sig).astype(BF16)
+        g = (ups[local, :] * sig * (1.0 + p * (1.0 - sig))).astype(BF16)
+        sg[pl.ds(pl.multiple_of((i + 2) * 128, 128), 128), :] = (
+            g.astype(F32) * lanes(root, 256)
+        ).astype(BF16)
+
+    g_core = []
+    for xb in range(2):
+        prop(sh, 256, xb, emit_h, before_h)
+        block = grid_rows(sg, (xb * 2 + c) * 8, 8)
+        g_core.append(send(block, block, {"tile": core}))
+    gs[...] = dot(act[...], back[...], TN)
+    for copy in g_core:
+        copy.wait_recv()
+
+    def emit_send(lr, i, at, local, ch, root, value):
+        fsend[pl.ds(pl.multiple_of(lr * 128, 128), 128), :] = value.astype(BF16)
+
+    def emit_keep(lr, i, at, local, ch, root, value):
+        first[x, pl.ds(pl.multiple_of(lr * 128, 128), 128), :] = value.astype(BF16)
+
+    prop(sg, 256, 1 - x, emit_send)
+    f_x = send(fsend, first.at[x], {"tile": other})
+    prop(sg, 256, x, emit_keep)
+
+    def xt(j):
+        def step(g, _):
+            rows = pl.ds(pl.multiple_of(g * 256, 256), 256)
+            gf[j, rows, :] = dot(x_ref[:, pl.ds(pl.multiple_of(g * 256, 256), 256)], first[j], TN)
+            return 0
+
+        lax.fori_loop(0, 4, step, 0)
+
+    xt(x)
+    f_x.wait_recv()
+    xt(1 - x)
+
+    up, low = (1 - c) * 512, c * 512
+    gfb[...] = gf[:, pl.ds(pl.multiple_of(up, 512), 512), :].astype(BF16)
+    gsb[...] = gs[pl.ds(pl.multiple_of((1 - c) * 128, 128), 128), :].astype(BF16)
+    s1 = send(gfb, gfr, {"tile": core})
+    s2 = send(gsb, gsr, {"tile": core})
+
+    def feats(g, _):
+        rows = pl.ds(pl.multiple_of(g * 256, 256), 256)
+        out_ref[rows, :] = (
+            dot(first[0, rows, :], w1_ref[:, 0:256], NT)
+            + dot(first[1, rows, :], w1_ref[:, 256:512], NT)
+        ).astype(BF16)
+        return 0
+
+    s1.wait_recv()
+    s2.wait_recv()
+    theirs = pl.multiple_of(low + (1 - x) * 256, 256)
+    ours = pl.multiple_of(low + x * 256, 256)
+    rtheirs = pl.multiple_of((1 - x) * 256, 256)
+    rours = pl.multiple_of(x * 256, 256)
+    gfx[...] = (
+        gf[:, pl.ds(theirs, 256), :] + gfr[:, pl.ds(rtheirs, 256), :].astype(F32)
+    ).astype(BF16)
+    s3 = send(gfx, gfxr, {"tile": other})
+    gs_mine = gs[pl.ds(pl.multiple_of(c * 128, 128), 128), :] + gsr[...].astype(F32)
+    gsz[...] = gs_mine.astype(BF16)
+    s4 = []
+    for k, peer in enumerate(zs):
+        s4.append(
+            send(gsz.at[pl.ds(pl.multiple_of(peer * 32, 32), 32), :], gszr.at[k], {"dp": peer})
+        )
+    lax.fori_loop(0, 4, feats, 0)
+    s3.wait_recv()
+    gf[:, pl.ds(ours, 256), :] = (
+        gf[:, pl.ds(ours, 256), :]
+        + gfr[:, pl.ds(rours, 256), :].astype(F32)
+        + gfxr[...].astype(F32)
+    )
+    gfz[...] = gf[:, pl.ds(ours, 256), :].astype(BF16)
+    s5 = []
+    for k, peer in enumerate(zs):
+        s5.append(
+            send(gfz.at[:, pl.ds(pl.multiple_of(peer * 64, 64), 64), :], gfzr.at[k], {"dp": peer})
+        )
+    for copy in s4:
+        copy.wait_recv()
+    srow = pl.multiple_of(z * 32, 32)
+    total = gsz[pl.ds(srow, 32), :].astype(F32)
+    for k in range(3):
+        total = total + gszr[k].astype(F32)
+    gs_at = pl.multiple_of(x * 256 + c * 128, 128)
+    gs_ref[pl.ds(pl.multiple_of(gs_at + z * 32, 32), 32), :] = total.astype(BF16)
+    piece = gs_ref.at[pl.ds(pl.multiple_of(gs_at + z * 32, 32), 32), :]
+    s6 = [send(piece, piece, {"dp": peer}) for peer in zs]
+    for copy in s5:
+        copy.wait_recv()
+    total = gf[:, pl.ds(pl.multiple_of(ours + z * 64, 64), 64), :]
+    for k in range(3):
+        total = total + gfzr[k].astype(F32)
+    gf_ref[:, pl.ds(pl.multiple_of(ours + z * 64, 64), 64), :] = total.astype(BF16)
+    piece = gf_ref.at[:, pl.ds(pl.multiple_of(ours + z * 64, 64), 64), :]
+    s7 = [send(piece, piece, {"dp": peer}) for peer in zs]
+    for copy in s6:
+        copy.wait_recv()
+    piece = gs_ref.at[pl.ds(gs_at, 128), :]
+    s8 = send(piece, piece, {"tile": other})
+    for copy in s7:
+        copy.wait_recv()
+    piece = gf_ref.at[:, pl.ds(ours, 256), :]
+    s9 = send(piece, piece, {"tile": other})
+    s8.wait_recv()
+    s10 = []
+    for xb in range(2):
+        piece = gs_ref.at[pl.ds(pl.multiple_of(xb * 256 + c * 128, 128), 128), :]
+        s10.append(send(piece, piece, {"tile": core}))
+    s9.wait_recv()
+    piece = gf_ref.at[:, pl.ds(pl.multiple_of(low, 512), 512), :]
+    s11 = send(piece, piece, {"tile": core})
+    for copy in s10:
+        copy.wait_recv()
+    s11.wait_recv()
+    flush()
+
+
+def fused(features, cotangent, weight_first, weight_second, cluster_id, cluster_size):
+    vm = pltpu.VMEM
+    scratch = [
+        vm((32, 128), jnp.int32), vm((2048, 4096), BF16), vm((2048, 128), F32),
+        vm((4608, 512), BF16), vm((4608, 256), BF16), vm((4608, 256), BF16),
+        vm((2, 1024, 256), BF16), vm((2048, 512), BF16), vm((2048, 256), BF16),
+        vm((512, 512), F32), vm((512, 256), F32), vm((2, 1024, 256), BF16),
+        vm((1024, 256), BF16), vm((2, 1024, 256), F32), vm((256, 512), F32),
+        vm((2, 512, 256), BF16), vm((128, 512), BF16), vm((2, 512, 256), BF16),
+        vm((128, 512), BF16), vm((2, 256, 256), BF16), vm((2, 256, 256), BF16),
+        vm((2, 256, 256), BF16), vm((128, 512), BF16), vm((3, 2, 64, 256), BF16),
+        vm((3, 32, 512), BF16), pltpu.SemaphoreType.DMA((40,)), pltpu.SemaphoreType.DMA((40,)),
+    ]
+    spec = pl.BlockSpec(memory_space=pltpu.VMEM)
+    feats, first, second = pl.pallas_call(
+        kernel,
+        out_shape=(
+            jax.ShapeDtypeStruct((1024, 1024), BF16),
+            jax.ShapeDtypeStruct((2, 1024, 256), BF16),
+            jax.ShapeDtypeStruct((512, 512), BF16),
+        ),
+        in_specs=[spec] * 5,
+        out_specs=(spec,) * 3,
+        scratch_shapes=scratch,
+        compiler_params=pltpu.CompilerParams(
+            collective_id=0, has_side_effects=True, vmem_limit_bytes=60 * 1024 * 1024
+        ),
+    )(
+        features.reshape(1024, 1024), cotangent.reshape(1024, 512),
+        weight_first, weight_second, cluster_id[0],
+    )
+    grad_first = jnp.concatenate([first[0], first[1]], axis=1).astype(F32)
+    return feats.reshape(features.shape), grad_first, second.astype(F32)
+
+
 def solution(mesh):
     in_specs = (
         P(("groups", "dp"), "tile", None, None),
@@ -123,4 +474,6 @@
         P(("groups", "dp"), None),
     )
     out_specs = (P(("groups", "dp"), "tile", None, None), P("groups", None), P("groups", None))
-    return jax.shard_map(local, mesh=mesh, in_specs=in_specs, out_specs=out_specs, check_vma=False)
+    sized = mesh.shape["tile"] == 4 and mesh.shape["dp"] == 4
+    body = fused if sized else local
+    return jax.shard_map(body, mesh=mesh, in_specs=in_specs, out_specs=out_specs, check_vma=False)

time: 262 us -> 119 us (0.45)
  waiting for transfers between devices: 141 us -> 0 us
  Pallas kernels: 0 us -> 112 us
  matrix products: 32.1 us -> 0 us
  starting transfers between devices: 30.9 us -> 0 us
  other arithmetic: 20.3 us -> 2.71 us
  between operations: 14.2 us -> 0.66 us
  local copies, waits for them, and re-layouts: 14.8 us -> 2.6 us
  blocking collectives: 7.36 us -> 0 us
    pallas_call x0 -> x1, Pallas kernels: none -> 112 us  [fused(): pl.pallas_call(kernel, out_shape=(jax.ShapeDtypeStruct((1024, 1024), BF16...]
    psum x1 -> x0, waiting for transfers between devices: 92.1 us -> none  [local(): lax.psum((grad_first.astype(jnp.bfloat16), grad_second.astype(jnp.bfloat1...]
    all_gather x3 -> x0, waiting for transfers between devices: 41.8 us -> none  [propagate(): piece_values = lax.all_gather(scaled, 'tile', axis=0, tiled=True)]
    dot_general x8 -> x0, matrix products: 32.1 us -> none  [the longest x3 20.6 us: propagate(): jnp.dot(same, piece_values.reshape(-1, width), preferred_element_type=jnp...]
    ppermute x12 -> x0, starting transfers between devices: 30.7 us -> none  [the longest x6 22.6 us: extended(): lax.ppermute(tail, axis, [(i, (i + 1) % count) for i in range(ends)])]
    add x6 -> x0, other arithmetic: 9.47 us -> none  [rowbox(): return values[:-2] + values[1:-1] + values[2:]]
    ppermute x12 -> x0, waiting for transfers between devices: 7.53 us -> none  [the longest x6 7.51 us: extended(): lax.ppermute(head, axis, [((i + 1) % count, i) for i in range(ends)])]
    all_gather x1 -> x0, blocking collectives: 7.36 us -> none  [local(): every = lax.all_gather(members, 'tile', axis=0, tiled=True)]
  transfers between devices with their start and end apart: 16 -> 0, of which waited for: 9 -> 0; matrix products, arithmetic and copies ran while one was open for 11% -> 0% of each run, Pallas kernels for 0% -> 0%
where the time goes in v2:
time: 119 us; the launch traced here: 118 us
  Pallas kernels  112 us (94%)
  other arithmetic  2.71 us (2%)
  local copies, waits for them, and re-layouts  2.6 us (2%)
    pallas_call x1, Pallas kernels, fused(): pl.pallas_call(kernel, out_shape=(jax.ShapeDtypeStruct((1024, 1024), BF16...  112 us

profile of v2, /device:TPU:0, one launch (start us, length us, event | category | flops | bytes accessed | tf_op | source)
XLA Modules:
  0.0 118.0 jit_solution(98554032710309740)
XLA Ops:
  0.6 112.0 %shard_map.76 = (bf16[1024,1024]{1,0:T(8,128)(2,1)}, bf16[2,1024,256]{2,1,0:T(8,128)(2,1)}, bf16[512,512]{1,0:T(8,128)(2,1)}) custom-call(bf16[1024,1024]{1,0:T(8,128)(2,1)} %bitcast.9, bf16[1024,512]{1,0:T(8,128)(2,1)} %bitcast.10, bf16[1024,512]{1,0:T(8,128)(2,1)} %w1_ref.1, bf16[512,512]{1,0:T(8,128)(2,1)} %w2_ref.1, s32[8,128]{1,0:T(8,128)} %bitcast.11), custom_call_target="tpu_custom_call" | custom-call | tf_op jit(solution)/shard_map/pallas_call | solution.py:446
  112.7 1.3 %slice_bitcast_fusion.1 = (bf16[1024,256]{1,0:T(8,128)(2,1)S(1)}, bf16[1024,256]{1,0:T(8,128)(2,1)S(1)}) fusion(bf16[2,1024,256]{2,1,0:T(8,128)(2,1)} %get-tuple-element.7), kind=kLoop, calls=%fused_computation.2 | loop fusion | bytes 2097152 | tf_op jit(solution)/shard_map/squeeze | solution.py:463
  113.9 0.0 copy-start.1
  113.9 0.0 copy-start
  114.0 1.6 %maximum_convert_fusion = f32[1024,512]{1,0:T(8,128)} fusion(bf16[1024,256]{1,0:T(8,128)(2,1)S(1)} %get-tuple-element.10, bf16[1024,256]{1,0:T(8,128)(2,1)S(1)} %get-tuple-element.9), kind=kLoop, calls=%fused_computation | loop fusion | flops 2097152 | bytes 3145728 | tf_op jit(solution)/shard_map/convert_element_type | solution.py:463
  115.6 0.0 copy-done.1
  115.6 1.1 convert_element_type.7
  116.7 0.0 copy-done
  116.7 1.3 %copy.9 = bf16[1,8,128,1024]{3,2,1,0:T(8,128)(2,1)} copy(bf16[1,8,128,1024]{3,2,1,0:T(8,128)(2,1)S(1)} %bitcast.8) | data formatting | bytes 4194304
Async XLA Ops:
  113.9 1.6 %copy-start.1 = (bf16[512,512]{1,0:T(8,128)(2,1)S(1)}, bf16[512,512]{1,0:T(8,128)(2,1)}, u32[]{:S(2)}) copy-start(bf16[512,512]{1,0:T(8,128)(2,1)} %get-tuple-element.8) | copy-start | bytes 1572868
  113.9 2.7 %copy-start = (bf16[1024,1024]{1,0:T(8,128)(2,1)S(1)}, bf16[1024,1024]{1,0:T(8,128)(2,1)}, u32[]{:S(2)}) copy-start(bf16[1024,1024]{1,0:T(8,128)(2,1)} %get-tuple-element.6) | copy-start | bytes 6291460

commit v3 on v2

--- a/solution.py
+++ b/solution.py
@@ -131,7 +131,7 @@
 
 def kernel(
     x_ref, c_ref, w1_ref, w2_ref, id_ref, out_ref, gf_ref, gs_ref,
-    ids, same, rcnt, sc, sh, sg, hs, back, act, tot, ups, first, fsend,
+    ids, same, rcnt, sc, sh, sg, hs, back, act, slope, first, fsend,
     gf, gs, gfb, gsb, gfr, gsr, gfx, gfxr, gfz, gsz, gfzr, gszr, sends, recvs,
 ):
     t = lax.axis_index("tile")
@@ -186,25 +186,25 @@
     def scale_c(r, _):
         i = t * 8 + r
         v = c_ref[pl.ds(pl.multiple_of(r * 128, 128), 128), :].astype(F32)
-        sc[pl.ds(pl.multiple_of((i + 2) * 128, 128), 128), :] = (
-            v * lanes(root_of(i), 512)
-        ).astype(BF16)
+        v = (v * lanes(root_of(i), 512)).astype(BF16)
+        for j in range(2):
+            sc[j, pl.ds(pl.multiple_of((i + 2) * 128, 128), 128), :] = v[:, j * 256 : j * 256 + 256]
         return 0
 
     lax.fori_loop(0, 8, scale_c, 0)
-    for ref in (sc, sh, sg):
+    for ref in (sc.at[0], sc.at[1], sh, sg):
         ref[0:256, :] = jnp.zeros((256, ref.shape[1]), BF16)
         ref[4352:4608, :] = jnp.zeros((256, ref.shape[1]), BF16)
 
     pl.semaphore_wait(barrier, 6)
     mine = ids.at[pl.ds(pl.multiple_of(t * 8, 8), 8), :]
     id_copies = [send(mine, mine, {"tile": p}) for p in (other, core, diag)]
-    cx = []
-    for part in range(4):
-        block = grid_rows(sc, t * 8 + part * 2, 2)
-        cx.append(send(block, block, {"tile": other}, False))
-    own = grid_rows(sc, t * 8, 8)
-    c_core = send(own, own, {"tile": core})
+    def send_c(j, where, band, track=True):
+        blocks = [grid_rows(sc.at[j], band * 8 + part * 4, 4) for part in range(2)]
+        return [send(block, block, {"tile": where}, track) for block in blocks]
+
+    cx = send_c(0, other, t, False)
+    c_core = send_c(0, core, t) + send_c(1, core, t)
 
     def hidden(g, _):
         rows = pl.ds(pl.multiple_of(g * 256, 256), 256)
@@ -219,6 +219,7 @@
     lax.fori_loop(0, 4, hidden, 0)
     rows_h = grid_rows(sh, t * 8, 8)
     h_core = send(hs.at[x], rows_h, {"tile": core})
+    h_x = send(hs.at[1 - x], rows_h, {"tile": other})
     sh[pl.ds(pl.multiple_of((t * 8 + 2) * 128, 128), 1024), :] = hs[x]
 
     for copy in id_copies:
@@ -239,99 +240,118 @@
 
     lax.fori_loop(0, 16, build, 0)
 
-    def prop(src, width, xb, emit, before=None):
+    def prop_group(src, xb, g, emit):
+        total = dot(same[pl.ds(pl.multiple_of(xb * 1024 + g * 512, 512), 512), :], src[256:4352, :])
+        colw = lanes(col, 256)
+
+        def colbox(u):
+            up = jnp.where(colw == 0, 0.0, pltpu.roll(u, 1, 0))
+            down = jnp.where(colw == 127, 0.0, pltpu.roll(u, 127, 0))
+            return u + up + down
+
+        for r in range(4):
+            lr = g * 4 + r
+            i = (xb * 2 + c) * 8 + lr
+            qs = [q_of(i - 1), q_of(i), q_of(i + 1)]
+            taps = [qs[0], qs[0] + qs[1], qs[0] + qs[1] + qs[2], qs[1] + qs[2], qs[2]]
+            at = pl.ds(pl.multiple_of(xb * 1024 + lr * 128, 128), 128)
+            v = jnp.zeros((128, 256), F32)
+            for k in range(5):
+                rowk = src[pl.ds(pl.multiple_of((i + k) * 128, 128), 128), :]
+                v = v + taps[k] * rowk.astype(F32)
+            v = colbox(colbox(v) * lanes(1.0 / cp, 256))
+            mean = (total[r * 128 : r * 128 + 128] * lanes(rcnt[at, :], 256)).astype(BF16)
+            emit(lr, i, at, lanes(root_of(i), 256) * (v + mean.astype(F32)))
+
+    def prop(src, xb, emit):
         def group(g, _):
-            rows = pl.ds(pl.multiple_of(xb * 1024 + g * 512, 512), 512)
-            tot[:, :width] = dot(same[rows, :], src[256:4352, :])
-            if before is not None:
-                before(rows)
-
-            def one(r, _):
-                lr = g * 4 + r
-                i = (xb * 2 + c) * 8 + lr
-                qs = [q_of(i - 1), q_of(i), q_of(i + 1)]
-                taps = [qs[0], qs[0] + qs[1], qs[0] + qs[1] + qs[2], qs[1] + qs[2], qs[2]]
-                local = pl.ds(pl.multiple_of(r * 128, 128), 128)
-                at = pl.ds(pl.multiple_of(xb * 1024 + lr * 128, 128), 128)
-                root = root_of(i)
-                for w in range(0, width, 256):
-                    ch = slice(w, w + 256)
-                    v = jnp.zeros((128, 256), F32)
-                    for k in range(5):
-                        rowk = src[pl.ds(pl.multiple_of((i + k) * 128, 128), 128), ch]
-                        v = v + taps[k] * rowk.astype(F32)
-                    colw = lanes(col, 256)
-
-                    def colbox(u):
-                        up = jnp.where(colw == 0, 0.0, pltpu.roll(u, 1, 0))
-                        down = jnp.where(colw == 127, 0.0, pltpu.roll(u, 127, 0))
-                        return u + up + down
-
-                    v = colbox(colbox(v) * lanes(1.0 / cp, 256))
-                    mean = (tot[local, ch] * lanes(rcnt[at, :], 256)).astype(BF16)
-                    emit(lr, i, at, local, ch, root, lanes(root, 256) * (v + mean.astype(F32)))
-                return 0
-
-            lax.fori_loop(0, 4, one, 0)
+            prop_group(src, xb, g, emit)
             return 0
 
         lax.fori_loop(0, 2, group, 0)
 
-    fw = []
-    for part in range(4):
-        cx[part].wait_recv()
-        block = grid_rows(sc, other * 8 + part * 2, 2)
-        fw.append(send(block, block, {"tile": core}))
-    for part in range(4):
-        cx[part].wait_send()
-    h_x = send(hs.at[1 - x], rows_h, {"tile": other})
-    c_core.wait_recv()
-    for copy in fw:
-        copy.wait_recv()
-
-    def emit_c(lr, i, at, local, ch, root, value):
-        back[at, ch] = value.astype(BF16)
-
-    prop(sc, 512, 0, emit_c)
-    prop(sc, 512, 1, emit_c)
-
+    def prop_both(src, emit):
+        def group(g, _):
+            prop_group(src, g // 2, g % 2, emit)
+            return 0
+
+        lax.fori_loop(0, 4, group, 0)
+
+    def forward_c(j, copies):
+        out = []
+        for part in range(2):
+            copies[part].wait_recv()
+            block = grid_rows(sc.at[j], other * 8 + part * 4, 4)
+            out.append(send(block, block, {"tile": core}))
+        for copy in out:
+            copy.wait_recv()
+
+    for copy in cx:
+        copy.wait_send()
+    cy = send_c(1, other, t)
+    for copy in c_core:
+        copy.wait_recv()
+    forward_c(0, cx)
+
+    def emit_c(j):
+        def emit(lr, i, at, value):
+            back[at, j * 256 : j * 256 + 256] = value.astype(BF16)
+
+        return emit
+
+    prop_both(sc.at[0], emit_c(0))
     h_x.wait_recv()
     block = grid_rows(sh, other * 8, 8)
     h_fw = send(block, block, {"tile": core})
     h_core.wait_recv()
     h_fw.wait_recv()
 
-    def before_h(rows):
-        half = w2_ref[pl.ds(pl.multiple_of(x * 256, 256), 256), :]
-        ups[...] = dot(back[rows, :], half, NT)
-
-    def emit_h(lr, i, at, local, ch, root, value):
+    def emit_h(lr, i, at, value):
         p = value.astype(BF16).astype(F32)
         sig = 1.0 / (1.0 + jnp.exp(-p))
         act[at, :] = (p * sig).astype(BF16)
-        g = (ups[local, :] * sig * (1.0 + p * (1.0 - sig))).astype(BF16)
-        sg[pl.ds(pl.multiple_of((i + 2) * 128, 128), 128), :] = (
-            g.astype(F32) * lanes(root, 256)
-        ).astype(BF16)
+        slope[at, :] = sig * (1.0 + p * (1.0 - sig))
+
+    prop_both(sh, emit_h)
+    forward_c(1, cy)
+
+    def upstream(xb):
+        half = w2_ref[pl.ds(pl.multiple_of(x * 256, 256), 256), :]
+
+        def step(g, _):
+            rows = pl.ds(pl.multiple_of(xb * 1024 + g * 256, 256), 256)
+            grad = (dot(back[rows, :], half, NT) * slope[rows, :]).astype(BF16).astype(F32)
+            for k in range(2):
+                i = (xb * 2 + c) * 8 + g * 2 + k
+                sg[pl.ds(pl.multiple_of((i + 2) * 128, 128), 128), :] = (
+                    grad[k * 128 : k * 128 + 128] * lanes(root_of(i), 256)
+                ).astype(BF16)
+            return 0
+
+        lax.fori_loop(0, 4, step, 0)
 
     g_core = []
     for xb in range(2):
-        prop(sh, 256, xb, emit_h, before_h)
+        prop(sc.at[1], xb, emit_c(1))
+        upstream(xb)
         block = grid_rows(sg, (xb * 2 + c) * 8, 8)
         g_core.append(send(block, block, {"tile": core}))
     gs[...] = dot(act[...], back[...], TN)
     for copy in g_core:
         copy.wait_recv()
 
-    def emit_send(lr, i, at, local, ch, root, value):
+    def emit_send(lr, i, at, value):
         fsend[pl.ds(pl.multiple_of(lr * 128, 128), 128), :] = value.astype(BF16)
 
-    def emit_keep(lr, i, at, local, ch, root, value):
+    def emit_keep(lr, i, at, value):
         first[x, pl.ds(pl.multiple_of(lr * 128, 128), 128), :] = value.astype(BF16)
 
-    prop(sg, 256, 1 - x, emit_send)
-    f_x = send(fsend, first.at[x], {"tile": other})
-    prop(sg, 256, x, emit_keep)
+    f_x = []
+    for g in range(2):
+        prop_group(sg, 1 - x, g, emit_send)
+        part = pl.ds(g * 512, 512)
+        f_x.append(send(fsend.at[part, :], first.at[x, part, :], {"tile": other}))
+    prop(sg, x, emit_keep)
 
     def xt(j):
         def step(g, _):
@@ -342,7 +362,8 @@
         lax.fori_loop(0, 4, step, 0)
 
     xt(x)
-    f_x.wait_recv()
+    for copy in f_x:
+        copy.wait_recv()
     xt(1 - x)
 
     up, low = (1 - c) * 512, c * 512
@@ -404,8 +425,10 @@
     total = gf[:, pl.ds(pl.multiple_of(ours + z * 64, 64), 64), :]
     for k in range(3):
         total = total + gfzr[k].astype(F32)
-    gf_ref[:, pl.ds(pl.multiple_of(ours + z * 64, 64), 64), :] = total.astype(BF16)
-    piece = gf_ref.at[:, pl.ds(pl.multiple_of(ours + z * 64, 64), 64), :]
+    gf_ref[pl.ds(pl.multiple_of(ours + z * 64, 64), 64), :] = jnp.concatenate(
+        [total[0], total[1]], axis=1
+    ).astype(BF16)
+    piece = gf_ref.at[pl.ds(pl.multiple_of(ours + z * 64, 64), 64), :]
     s7 = [send(piece, piece, {"dp": peer}) for peer in zs]
     for copy in s6:
         copy.wait_recv()
@@ -413,7 +436,7 @@
     s8 = send(piece, piece, {"tile": other})
     for copy in s7:
         copy.wait_recv()
-    piece = gf_ref.at[:, pl.ds(ours, 256), :]
+    piece = gf_ref.at[pl.ds(ours, 256), :]
     s9 = send(piece, piece, {"tile": other})
     s8.wait_recv()
     s10 = []
@@ -421,7 +444,7 @@
         piece = gs_ref.at[pl.ds(pl.multiple_of(xb * 256 + c * 128, 128), 128), :]
         s10.append(send(piece, piece, {"tile": core}))
     s9.wait_recv()
-    piece = gf_ref.at[:, pl.ds(pl.multiple_of(low, 512), 512), :]
+    piece = gf_ref.at[pl.ds(pl.multiple_of(low, 512), 512), :]
     s11 = send(piece, piece, {"tile": core})
     for copy in s10:
         copy.wait_recv()
@@ -433,21 +456,21 @@
     vm = pltpu.VMEM
     scratch = [
         vm((32, 128), jnp.int32), vm((2048, 4096), BF16), vm((2048, 128), F32),
-        vm((4608, 512), BF16), vm((4608, 256), BF16), vm((4608, 256), BF16),
+        vm((2, 4608, 256), BF16), vm((4608, 256), BF16), vm((4608, 256), BF16),
         vm((2, 1024, 256), BF16), vm((2048, 512), BF16), vm((2048, 256), BF16),
-        vm((512, 512), F32), vm((512, 256), F32), vm((2, 1024, 256), BF16),
+        vm((2048, 256), F32), vm((2, 1024, 256), BF16),
         vm((1024, 256), BF16), vm((2, 1024, 256), F32), vm((256, 512), F32),
         vm((2, 512, 256), BF16), vm((128, 512), BF16), vm((2, 512, 256), BF16),
         vm((128, 512), BF16), vm((2, 256, 256), BF16), vm((2, 256, 256), BF16),
         vm((2, 256, 256), BF16), vm((128, 512), BF16), vm((3, 2, 64, 256), BF16),
-        vm((3, 32, 512), BF16), pltpu.SemaphoreType.DMA((40,)), pltpu.SemaphoreType.DMA((40,)),
+        vm((3, 32, 512), BF16), pltpu.SemaphoreType.DMA((48,)), pltpu.SemaphoreType.DMA((48,)),
     ]
     spec = pl.BlockSpec(memory_space=pltpu.VMEM)
     feats, first, second = pl.pallas_call(
         kernel,
         out_shape=(
             jax.ShapeDtypeStruct((1024, 1024), BF16),
-            jax.ShapeDtypeStruct((2, 1024, 256), BF16),
+            jax.ShapeDtypeStruct((1024, 512), BF16),
             jax.ShapeDtypeStruct((512, 512), BF16),
         ),
         in_specs=[spec] * 5,
@@ -460,8 +483,7 @@
         features.reshape(1024, 1024), cotangent.reshape(1024, 512),
         weight_first, weight_second, cluster_id[0],
     )
-    grad_first = jnp.concatenate([first[0], first[1]], axis=1).astype(F32)
-    return feats.reshape(features.shape), grad_first, second.astype(F32)
+    return feats.reshape(features.shape), first.astype(F32), second.astype(F32)
 
 
 def solution(mesh):

time: 119 us -> 113 us (0.950)
  Pallas kernels: 112 us -> 107 us
  other arithmetic: 2.71 us -> 4.09 us
  local copies, waits for them, and re-layouts: 2.6 us -> 1.33 us
    pallas_call x1, Pallas kernels: 112 us -> 107 us  [fused(): pl.pallas_call(kernel, out_shape=(jax.ShapeDtypeStruct((1024, 1024), BF16...]
    convert_element_type x2, other arithmetic: 2.71 us -> 4.09 us  [the longest x1 2.99 us: fused(): first.astype(F32)]
    squeeze x1 -> x0, local copies, waits for them, and re-layouts: 1.27 us -> none  [fused(): grad_first = jnp.concatenate([first[0], first[1]], axis=1).astype(F32)]
where the time goes in v3:
time: 113 us
  Pallas kernels  107 us (95%)
  other arithmetic  4.09 us (4%)
  local copies, waits for them, and re-layouts  1.33 us (1%)
    pallas_call x1, Pallas kernels, fused(): pl.pallas_call(kernel, out_shape=(jax.ShapeDtypeStruct((1024, 1024), BF16...  107 us
    convert_element_type x1, other arithmetic, fused(): first.astype(F32)  2.99 us

profile of v3, /device:TPU:0, one launch (start us, length us, event | category | flops | bytes accessed | tf_op | source)
XLA Modules:
  0.0 112.6 jit_solution(14195179742079437251)
XLA Ops:
  0.6 106.5 %shard_map.76 = (bf16[1024,1024]{1,0:T(8,128)(2,1)}, bf16[1024,512]{1,0:T(8,128)(2,1)}, bf16[512,512]{1,0:T(8,128)(2,1)}) custom-call(bf16[1024,1024]{1,0:T(8,128)(2,1)} %bitcast.5, bf16[1024,512]{1,0:T(8,128)(2,1)} %bitcast.6, bf16[1024,512]{1,0:T(8,128)(2,1)} %w1_ref.1, bf16[512,512]{1,0:T(8,128)(2,1)} %w2_ref.1, s32[8,128]{1,0:T(8,128)} %bitcast.7), custom_call_target="tpu_custom_call" | custom-call | tf_op jit(solution)/shard_map/pallas_call | solution.py:469
  107.2 0.0 copy-start.1
  107.2 0.0 copy-start
  107.2 3.0 %convert_element_type.6 = f32[1024,512]{1,0:T(8,128)} convert(bf16[1024,512]{1,0:T(8,128)(2,1)} %get-tuple-element.7) | non-fusion elementwise | flops 524288 | bytes 3145728 | tf_op jit(solution)/shard_map/convert_element_type | solution.py:486
  110.2 0.0 copy-done.1
  110.2 1.1 convert_element_type.7
  111.3 0.0 copy-done
  111.3 1.3 %copy.9 = bf16[1,8,128,1024]{3,2,1,0:T(8,128)(2,1)} copy(bf16[1,8,128,1024]{3,2,1,0:T(8,128)(2,1)S(1)} %bitcast.4) | data formatting | bytes 4194304
Async XLA Ops:
  107.2 3.0 %copy-start.1 = (bf16[512,512]{1,0:T(8,128)(2,1)S(1)}, bf16[512,512]{1,0:T(8,128)(2,1)}, u32[]{:S(2)}) copy-start(bf16[512,512]{1,0:T(8,128)(2,1)} %get-tuple-element.8) | copy-start | bytes 1572868
  107.2 4.1 %copy-start = (bf16[1024,1024]{1,0:T(8,128)(2,1)S(1)}, bf16[1024,1024]{1,0:T(8,128)(2,1)}, u32[]{:S(2)}) copy-start(bf16[1024,1024]{1,0:T(8,128)(2,1)} %get-tuple-element.6) | copy-start | bytes 6291460

commit v4 on v3

--- a/solution.py
+++ b/solution.py
@@ -337,8 +337,18 @@
         block = grid_rows(sg, (xb * 2 + c) * 8, 8)
         g_core.append(send(block, block, {"tile": core}))
     gs[...] = dot(act[...], back[...], TN)
+    gsb[...] = gs[pl.ds(pl.multiple_of((1 - c) * 128, 128), 128), :].astype(BF16)
+    s2 = send(gsb, gsr, {"tile": core})
     for copy in g_core:
         copy.wait_recv()
+    s2.wait_recv()
+    gs_mine = gs[pl.ds(pl.multiple_of(c * 128, 128), 128), :] + gsr[...].astype(F32)
+    gsz[...] = gs_mine.astype(BF16)
+    s4 = []
+    for k, peer in enumerate(zs):
+        s4.append(
+            send(gsz.at[pl.ds(pl.multiple_of(peer * 32, 32), 32), :], gszr.at[k], {"dp": peer})
+        )
 
     def emit_send(lr, i, at, value):
         fsend[pl.ds(pl.multiple_of(lr * 128, 128), 128), :] = value.astype(BF16)
@@ -351,7 +361,20 @@
         prop_group(sg, 1 - x, g, emit_send)
         part = pl.ds(g * 512, 512)
         f_x.append(send(fsend.at[part, :], first.at[x, part, :], {"tile": other}))
+    for copy in s4:
+        copy.wait_recv()
+    total = gsz[pl.ds(pl.multiple_of(z * 32, 32), 32), :].astype(F32)
+    for k in range(3):
+        total = total + gszr[k].astype(F32)
+    gs_at = pl.multiple_of(x * 256 + c * 128, 128)
+    gs_ref[pl.ds(pl.multiple_of(gs_at + z * 32, 32), 32), :] = total.astype(BF16)
+    piece = gs_ref.at[pl.ds(pl.multiple_of(gs_at + z * 32, 32), 32), :]
+    s6 = [send(piece, piece, {"dp": peer}) for peer in zs]
     prop(sg, x, emit_keep)
+    for copy in s6:
+        copy.wait_recv()
+    piece = gs_ref.at[pl.ds(gs_at, 128), :]
+    s8 = send(piece, piece, {"tile": other})
 
     def xt(j):
         def step(g, _):
@@ -367,10 +390,10 @@
     xt(1 - x)
 
     up, low = (1 - c) * 512, c * 512
-    gfb[...] = gf[:, pl.ds(pl.multiple_of(up, 512), 512), :].astype(BF16)
-    gsb[...] = gs[pl.ds(pl.multiple_of((1 - c) * 128, 128), 128), :].astype(BF16)
-    s1 = send(gfb, gfr, {"tile": core})
-    s2 = send(gsb, gsr, {"tile": core})
+    s1 = []
+    for j in range(2):
+        gfb[j] = gf[j, pl.ds(pl.multiple_of(up, 512), 512), :].astype(BF16)
+        s1.append(send(gfb.at[j], gfr.at[j], {"tile": core}))
 
     def feats(g, _):
         rows = pl.ds(pl.multiple_of(g * 256, 256), 256)
@@ -380,75 +403,60 @@
         ).astype(BF16)
         return 0
 
-    s1.wait_recv()
-    s2.wait_recv()
-    theirs = pl.multiple_of(low + (1 - x) * 256, 256)
-    ours = pl.multiple_of(low + x * 256, 256)
-    rtheirs = pl.multiple_of((1 - x) * 256, 256)
-    rours = pl.multiple_of(x * 256, 256)
-    gfx[...] = (
-        gf[:, pl.ds(theirs, 256), :] + gfr[:, pl.ds(rtheirs, 256), :].astype(F32)
-    ).astype(BF16)
-    s3 = send(gfx, gfxr, {"tile": other})
-    gs_mine = gs[pl.ds(pl.multiple_of(c * 128, 128), 128), :] + gsr[...].astype(F32)
-    gsz[...] = gs_mine.astype(BF16)
-    s4 = []
-    for k, peer in enumerate(zs):
-        s4.append(
-            send(gsz.at[pl.ds(pl.multiple_of(peer * 32, 32), 32), :], gszr.at[k], {"dp": peer})
-        )
-    lax.fori_loop(0, 4, feats, 0)
-    s3.wait_recv()
-    gf[:, pl.ds(ours, 256), :] = (
-        gf[:, pl.ds(ours, 256), :]
-        + gfr[:, pl.ds(rours, 256), :].astype(F32)
-        + gfxr[...].astype(F32)
-    )
-    gfz[...] = gf[:, pl.ds(ours, 256), :].astype(BF16)
-    s5 = []
-    for k, peer in enumerate(zs):
-        s5.append(
-            send(gfz.at[:, pl.ds(pl.multiple_of(peer * 64, 64), 64), :], gfzr.at[k], {"dp": peer})
-        )
-    for copy in s4:
-        copy.wait_recv()
-    srow = pl.multiple_of(z * 32, 32)
-    total = gsz[pl.ds(srow, 32), :].astype(F32)
-    for k in range(3):
-        total = total + gszr[k].astype(F32)
-    gs_at = pl.multiple_of(x * 256 + c * 128, 128)
-    gs_ref[pl.ds(pl.multiple_of(gs_at + z * 32, 32), 32), :] = total.astype(BF16)
-    piece = gs_ref.at[pl.ds(pl.multiple_of(gs_at + z * 32, 32), 32), :]
-    s6 = [send(piece, piece, {"dp": peer}) for peer in zs]
-    for copy in s5:
-        copy.wait_recv()
-    total = gf[:, pl.ds(pl.multiple_of(ours + z * 64, 64), 64), :]
-    for k in range(3):
-        total = total + gfzr[k].astype(F32)
-    gf_ref[pl.ds(pl.multiple_of(ours + z * 64, 64), 64), :] = jnp.concatenate(
-        [total[0], total[1]], axis=1
-    ).astype(BF16)
-    piece = gf_ref.at[pl.ds(pl.multiple_of(ours + z * 64, 64), 64), :]
-    s7 = [send(piece, piece, {"dp": peer}) for peer in zs]
-    for copy in s6:
-        copy.wait_recv()
-    piece = gs_ref.at[pl.ds(gs_at, 128), :]
-    s8 = send(piece, piece, {"tile": other})
-    for copy in s7:
-        copy.wait_recv()
-    piece = gf_ref.at[pl.ds(ours, 256), :]
-    s9 = send(piece, piece, {"tile": other})
+    theirs = pl.ds(pl.multiple_of(low + (1 - x) * 256, 256), 256)
+    ours = pl.ds(pl.multiple_of(low + x * 256, 256), 256)
+    rtheirs = pl.ds(pl.multiple_of((1 - x) * 256, 256), 256)
+    rours = pl.ds(pl.multiple_of(x * 256, 256), 256)
+    s3 = []
+    for j in range(2):
+        s1[j].wait_recv()
+        gfx[j] = (gf[j, theirs, :] + gfr[j, rtheirs, :].astype(F32)).astype(BF16)
+        s3.append(send(gfx.at[j], gfxr.at[j], {"tile": other}))
     s8.wait_recv()
     s10 = []
     for xb in range(2):
         piece = gs_ref.at[pl.ds(pl.multiple_of(xb * 256 + c * 128, 128), 128), :]
         s10.append(send(piece, piece, {"tile": core}))
-    s9.wait_recv()
-    piece = gf_ref.at[pl.ds(pl.multiple_of(low, 512), 512), :]
-    s11 = send(piece, piece, {"tile": core})
-    for copy in s10:
-        copy.wait_recv()
-    s11.wait_recv()
+    lax.fori_loop(0, 2, feats, 0)
+    s5 = []
+    for j in range(2):
+        s3[j].wait_recv()
+        gf[j, ours, :] = (
+            gf[j, ours, :] + gfr[j, rours, :].astype(F32) + gfxr[j].astype(F32)
+        )
+        gfz[j] = gf[j, ours, :].astype(BF16)
+        for k, peer in enumerate(zs):
+            part = pl.ds(pl.multiple_of(peer * 64, 64), 64)
+            s5.append(send(gfz.at[j, part, :], gfzr.at[k, j], {"dp": peer}))
+    lax.fori_loop(2, 4, feats, 0)
+    here = pl.ds(pl.multiple_of(low + x * 256 + z * 64, 64), 64)
+    s7 = []
+    for j in range(2):
+        ch = slice(j * 256, j * 256 + 256)
+        for copy in s5[j * 3 : j * 3 + 3]:
+            copy.wait_recv()
+        total = gf[j, here, :]
+        for k in range(3):
+            total = total + gfzr[k, j].astype(F32)
+        gf_ref[here, ch] = total.astype(BF16)
+        piece = gf_ref.at[here, ch]
+        s7.append([send(piece, piece, {"dp": peer}) for peer in zs])
+    s9 = []
+    for j in range(2):
+        for copy in s7[j]:
+            copy.wait_recv()
+        piece = gf_ref.at[ours, j * 256 : j * 256 + 256]
+        s9.append(send(piece, piece, {"tile": other}))
+    s11 = []
+    for j in range(2):
+        piece = gf_ref.at[ours, j * 256 : j * 256 + 256]
+        s11.append(send(piece, piece, {"tile": core}))
+    for j in range(2):
+        s9[j].wait_recv()
+        piece = gf_ref.at[theirs, j * 256 : j * 256 + 256]
+        s11.append(send(piece, piece, {"tile": core}))
+    for copy in s10 + s11:
+        copy.wait_recv()
     flush()
 
 
@@ -463,7 +471,7 @@
         vm((2, 512, 256), BF16), vm((128, 512), BF16), vm((2, 512, 256), BF16),
         vm((128, 512), BF16), vm((2, 256, 256), BF16), vm((2, 256, 256), BF16),
         vm((2, 256, 256), BF16), vm((128, 512), BF16), vm((3, 2, 64, 256), BF16),
-        vm((3, 32, 512), BF16), pltpu.SemaphoreType.DMA((48,)), pltpu.SemaphoreType.DMA((48,)),
+        vm((3, 32, 512), BF16), pltpu.SemaphoreType.DMA((64,)), pltpu.SemaphoreType.DMA((64,)),
     ]
     spec = pl.BlockSpec(memory_space=pltpu.VMEM)
     feats, first, second = pl.pallas_call(

time: 113 us -> 106 us (0.938)
  Pallas kernels: 107 us -> 99.5 us
    pallas_call x1, Pallas kernels: 107 us -> 99.5 us  [fused(): pl.pallas_call(kernel, out_shape=(jax.ShapeDtypeStruct((1024, 1024), BF16...]
where the time goes in v4:
time: 106 us
  Pallas kernels  99.5 us (94%)
  other arithmetic  4.09 us (4%)
  local copies, waits for them, and re-layouts  1.33 us (1%)
    pallas_call x1, Pallas kernels, fused(): pl.pallas_call(kernel, out_shape=(jax.ShapeDtypeStruct((1024, 1024), BF16...  99.5 us
    convert_element_type x1, other arithmetic, fused(): first.astype(F32)  2.99 us

profile of v4, /device:TPU:0, one launch (start us, length us, event | category | flops | bytes accessed | tf_op | source)
XLA Modules:
  0.0 105.6 jit_solution(824310504182284937)
XLA Ops:
  0.6 99.5 %shard_map.76 = (bf16[1024,1024]{1,0:T(8,128)(2,1)}, bf16[1024,512]{1,0:T(8,128)(2,1)}, bf16[512,512]{1,0:T(8,128)(2,1)}) custom-call(bf16[1024,1024]{1,0:T(8,128)(2,1)} %bitcast.5, bf16[1024,512]{1,0:T(8,128)(2,1)} %bitcast.6, bf16[1024,512]{1,0:T(8,128)(2,1)} %w1_ref.1, bf16[512,512]{1,0:T(8,128)(2,1)} %w2_ref.1, s32[8,128]{1,0:T(8,128)} %bitcast.7), custom_call_target="tpu_custom_call" | custom-call | tf_op jit(solution)/shard_map/pallas_call | solution.py:477
  100.2 0.0 copy-start.1
  100.2 0.0 copy-start
  100.2 3.0 %convert_element_type.6 = f32[1024,512]{1,0:T(8,128)} convert(bf16[1024,512]{1,0:T(8,128)(2,1)} %get-tuple-element.7) | non-fusion elementwise | flops 524288 | bytes 3145728 | tf_op jit(solution)/shard_map/convert_element_type | solution.py:494
  103.2 0.0 copy-done.1
  103.2 1.1 %convert_element_type.7 = f32[512,512]{1,0:T(8,128)} convert(bf16[512,512]{1,0:T(8,128)(2,1)S(1)} %copy-done.1) | non-fusion elementwise | flops 262144 | bytes 1572864 | tf_op jit(solution)/shard_map/convert_element_type | solution.py:494
  104.3 0.0 copy-done
  104.3 1.3 %copy.9 = bf16[1,8,128,1024]{3,2,1,0:T(8,128)(2,1)} copy(bf16[1,8,128,1024]{3,2,1,0:T(8,128)(2,1)S(1)} %bitcast.4) | data formatting | bytes 4194304
Async XLA Ops:
  100.2 3.0 %copy-start.1 = (bf16[512,512]{1,0:T(8,128)(2,1)S(1)}, bf16[512,512]{1,0:T(8,128)(2,1)}, u32[]{:S(2)}) copy-start(bf16[512,512]{1,0:T(8,128)(2,1)} %get-tuple-element.8) | copy-start | bytes 1572868
  100.2 4.1 %copy-start = (bf16[1024,1024]{1,0:T(8,128)(2,1)S(1)}, bf16[1024,1024]{1,0:T(8,128)(2,1)}, u32[]{:S(2)}) copy-start(bf16[1024,1024]{1,0:T(8,128)(2,1)} %get-tuple-element.6) | copy-start | bytes 6291460
